TPU v7x, 512 devices: a whole 4x8x8 slice. The times are simulated.
512 devices in a mesh: head: 8 (over x, core), outer: 16 (over y_hi, z), inner: 4 (over y_lo).
Axes of the slice: x: 4, y: 8 (y_hi: 2, y_lo: 4; y = y_hi * 4 + y_lo), z: 8, core: 2. Of those that a mesh axis runs over, the one named last changes fastest.
Arguments:
- queries: bfloat16 [8192, 24, 128], P(('outer', 'inner'), 'head'), may hold values from -9 to 9
- key_states: bfloat16 [64, 8, 16, 8, 128], P(('outer', 'inner'), 'head'), may hold values from -5 to 5
- value_states: bfloat16 [64, 8, 16, 8, 128], P(('outer', 'inner'), 'head'), may hold values from -6 to 6
- head_masks: int32 [24, 128, 128], P('head'), may hold values from 0 to 1, as said below
Outputs:
- attended: bfloat16 [8192, 24, 128], P(('outer', 'inner'), 'head')
Inputs may be any that keep to these rules, and one draw needn't show every extreme that they name: head_masks[h, i, j] is 0 for j > i and 1 for j = i and j = i - 1; other entries below the diagonal are 1 at a rate that differs by head.
All inputs are finite; a program needn't handle non-finite values.
Results may differ from a plain program's by a relative error of at most 0.0045.
Values may be sent and summed in bfloat16 or wider, within the bound.
No kernel may reach another device: no remote copies, remote signals or barrier semaphores. Data moves between devices by JAX's collectives and lax.ppermute only.
A program may use at most 128 MiB of HBM per device.

v0:
```python
import jax
import jax.numpy as jnp
from jax import lax
from jax.sharding import PartitionSpec as P


def online_step(running, query_block, key_piece, value_piece, allowed, score_scale):
    highest_old, denominator, weighted = running
    scores = (
        jnp.einsum("qkgd,ckd->kgqc", query_block, key_piece, preferred_element_type=jnp.float32)
        * score_scale
    )
    masked = jnp.where(allowed, scores, -1e30)
    highest = jnp.maximum(highest_old, jnp.max(masked, axis=3))
    weights = jnp.where(allowed, jnp.exp(masked - highest[..., None]), 0.0)
    denominator = jnp.sum(weights, axis=3)
    weighted = jnp.einsum(
        "kgqc,ckd->kgqd",
        weights.astype(jnp.bfloat16),
        value_piece,
        preferred_element_type=jnp.float32,
    )
    return (highest, denominator, weighted)


def per_device(queries, key_states, value_states, head_masks):
    key_part, value_part = (
        lax.all_to_all(key_states, "head", split_axis=3, concat_axis=1, tiled=True),
        lax.all_to_all(value_states, "head", split_axis=3, concat_axis=1, tiled=True),
    )
    tok_rows = queries.shape[0]
    heads_dev = queries.shape[1]
    head_dim = queries.shape[2]
    kv_dev = key_part.shape[3]
    per_group = heads_dev // kv_dev
    key_rows = key_part.reshape(tok_rows, kv_dev, head_dim)
    value_rows = value_part.reshape(tok_rows, kv_dev, head_dim)
    shard_count = lax.axis_size(("outer", "inner"))
    my_index = lax.axis_index(("outer", "inner"))
    block_len = tok_rows * shard_count // head_masks.shape[1]
    row_index = jnp.arange(tok_rows, dtype=jnp.int32)
    positions = my_index * tok_rows + row_index
    half_rows = tok_rows // 2
    query_halves = [
        queries[part_index * half_rows : (part_index + 1) * half_rows].reshape(
            half_rows, kv_dev, per_group, head_dim
        )
        for part_index in range(2)
    ]
    position_halves = [
        positions[part_index * half_rows : (part_index + 1) * half_rows] for part_index in range(2)
    ]
    mask_halves = [
        jnp.take(head_masks, where_rows // block_len, axis=1) for where_rows in position_halves
    ]
    score_scale = head_dim ** (-0.5)
    start_state = (
        jnp.full((kv_dev, per_group, half_rows), -1e30, jnp.float32),
        jnp.zeros((kv_dev, per_group, half_rows), jnp.float32),
        jnp.zeros((kv_dev, per_group, half_rows, head_dim), jnp.float32),
    )
    initial = (start_state, start_state)
    key_piece = lax.all_gather(key_rows, ("outer", "inner"), axis=0, tiled=True)
    value_piece = lax.all_gather(value_rows, ("outer", "inner"), axis=0, tiled=True)
    key_count = key_piece.shape[0]
    key_pos = jnp.arange(key_count, dtype=jnp.int32)
    updated = []
    for query_block, position_block, mask_block, running in zip(
        query_halves, position_halves, mask_halves, initial
    ):
        allowed = (jnp.repeat(mask_block, block_len, axis=2) > 0) & (
            position_block[:, None] >= key_pos[None, :]
        )
        allowed = allowed.reshape(kv_dev, per_group, half_rows, key_count)

        def advance(previous, query_block=query_block, allowed=allowed):
            return online_step(previous, query_block, key_piece, value_piece, allowed, score_scale)

        def unchanged(previous):
            return previous

        updated.append(lax.cond(jnp.any(allowed), advance, unchanged, running))
    finished = tuple(updated)
    outputs = []
    for highest, denominator, weighted in finished:
        normal = (weighted / denominator[..., None]).astype(jnp.bfloat16)
        outputs.append(normal.transpose(2, 0, 1, 3).reshape(half_rows, heads_dev, head_dim))
    attended = jnp.concatenate(outputs, axis=0)
    return attended


def solution(mesh):
    in_specs = (
        P(("outer", "inner"), "head", None),
        P(("outer", "inner"), "head", None, None, None),
        P(("outer", "inner"), "head", None, None, None),
        P("head", None, None),
    )
    out_specs = P(("outer", "inner"), "head", None)
    return jax.shard_map(
        per_device, mesh=mesh, in_specs=in_specs, out_specs=out_specs, check_vma=False
    )
```

profile of v0, /device:TPU:210, one launch (start us, length us, event | category | flops | bytes accessed | tf_op | source)
XLA Modules:
  0.0 672.6 jit_solution(16103627888904190484)
XLA Ops:
  6.5 0.0 copy-start
  6.5 0.0 all-gather.3.cloned.1.call-start
  6.5 0.8 copy.11
  7.3 8.7 %all_to_all.30 = bf16[1,1,16,8,128]{4,2,1,0,3:T(8,128)(2,1)} all-to-all(bf16[1,1,16,8,128]{4,2,1,0,3:T(8,128)(2,1)S(1)} %copy.11), channel_id=1, replica_groups=mesh['head'=8,'outer'=16,'inner'=4] {'head'}, dimensions={3} | all-to-all | bytes 65536 | tf_op jit(solution)/shard_map/all_to_all | solution.py:28
  16.1 0.0 all-gather.3.cloned.1.call-update
  16.1 0.0 all-gather.5.cloned.1.call-start
  16.1 0.8 copy.12
  16.9 8.5 %all_to_all.31 = bf16[1,1,16,8,128]{4,2,1,0,3:T(8,128)(2,1)} all-to-all(bf16[1,1,16,8,128]{4,2,1,0,3:T(8,128)(2,1)S(1)} %copy.12), channel_id=1, replica_groups=mesh['head'=8,'outer'=16,'inner'=4] {'head'}, dimensions={3} | all-to-all | bytes 65536 | tf_op jit(solution)/shard_map/all_to_all | solution.py:29
  25.4 0.0 all-gather.5.cloned.1.call-update
  25.4 0.1 compare_and_fusion.3
  25.5 0.0 copy-done
  25.5 0.7 gather_fusion
  26.3 0.7 gather_fusion.1
  27.0 0.1 fusion.40
  27.0 0.1 broadcast_compare_fusion.3
  27.1 0.1 broadcast_compare_fusion.2
  27.2 0.7 broadcast_compare_fusion.1
  27.9 2.4 and_reduce_fusion
  31.5 279.9 %all-gather.3.cloned.1.call-done = bf16[8192,1,128]{2,0,1:T(8,128)(2,1)} async-done(((bf16[128,1,128]{2,0,1:T(8,128)(2,1)}), bf16[8192,1,128]{2,0,1:T(8,128)(2,1)}) %all-gather.3.cloned.1.call-update) | async-done | bytes 2097168 | tf_op jit(solution)/shard_map/all_gather | solution.py:63
  311.5 294.5 %all-gather.5.cloned.1.call-done = bf16[8192,1,128]{2,0,1:T(8,128)(2,1)} async-done(((bf16[128,1,128]{2,0,1:T(8,128)(2,1)}), bf16[8192,1,128]{2,0,1:T(8,128)(2,1)}) %all-gather.5.cloned.1.call-update) | async-done | bytes 2097168 | tf_op jit(solution)/shard_map/all_gather | solution.py:64
  606.0 0.1 ge.79
  606.1 0.0 copy-start.6
  606.1 3.3 broadcast.98
  609.4 0.0 copy-done.6
  609.4 27.4 %conditional.2 = (f32[1,3,64]{2,1,0:T(4,128)S(1)}, f32[1,3,64,128]{3,2,1,0:T(8,128)S(1)}) conditional(s32[]{:T(128)} %convert_element_type.18, () %tuple.22, (s32[3,64,128]{2,1,0:T(8,128)S(1)}, s32[1,3,64,8192]{3,2,1,0:T(8,128)}, s32[64]{0:T(128)S(1)}, s32[1,64,8192]{2,1,0:T(8,128)S(1)}, bf16[8192,1,128]{2,0,1:T(8,128)(2,1)}, ...), branch_computations={%region_1.3_spmd, %region_2.0_spmd} | conditional | flops 823131968 | bytes 80991048 | solution.py:82
  609.4 5.5 broadcast_in_dim.50
  614.9 10.8 %reshape.123 = s32[1,3,64,8192]{3,2,1,0:T(8,128)} reshape(s32[3,64,128,64]{3,2,1,0:T(8,128)} %broadcast_in_dim.50) | data formatting | bytes 12582912 | tf_op jit(solution)/shard_map/reshape | solution.py:71
  625.7 0.3 compare_bitcast_fusion
  626.1 0.0 copy-start.2
  626.1 5.9 compare_and_fusion
  632.0 0.0 copy-done.2
  632.0 0.0 copy-start.4
  632.0 1.6 fusion.38
  633.6 0.0 copy-done.4
  633.6 1.7 fusion.11
  635.3 1.6 fusion.3
  636.9 0.1 fusion.36
  637.0 0.1 ge.82
  637.1 27.7 %conditional.3 = (f32[1,3,64]{2,1,0:T(4,128)S(1)}, f32[1,3,64,128]{3,2,1,0:T(8,128)S(1)}) conditional(s32[]{:T(128)} %convert_element_type.20, () %tuple.24, (s32[3,64,128]{2,1,0:T(8,128)S(1)}, s32[1,3,64,8192]{3,2,1,0:T(8,128)}, s32[64]{0:T(128)S(1)}, s32[1,64,8192]{2,1,0:T(8,128)S(1)}, bf16[8192,1,128]{2,0,1:T(8,128)(2,1)}, ...), branch_computations={%region_6.8_spmd, %region_7.11_spmd} | conditional | flops 823131968 | bytes 80991048 | solution.py:82
  637.3 5.6 broadcast_in_dim.56
  642.9 10.8 %reshape.127 = s32[1,3,64,8192]{3,2,1,0:T(8,128)} reshape(s32[3,64,128,64]{3,2,1,0:T(8,128)} %broadcast_in_dim.56) | data formatting | bytes 12582912 | tf_op jit(solution)/shard_map/reshape | solution.py:71
  653.7 0.3 compare_bitcast_fusion.1
  654.1 0.0 copy-start.3
  654.1 5.9 compare_and_fusion.1
  660.0 0.0 copy-done.3
  660.0 0.0 copy-start.5
  660.0 1.6 fusion.39
  661.6 0.0 copy-done.5
  661.6 1.7 fusion.29
  663.3 1.6 fusion.21
  664.9 0.0 copy-start.1
  664.9 0.1 fusion.37
  665.0 0.6 pad_maximum_fusion
  665.6 0.2 copy-done.1
  (6 shorter events, 0.0 us)
Async XLA Ops:
  6.5 19.0 %copy-start = (s32[3,128,128]{2,1,0:T(8,128)S(1)}, s32[3,128,128]{2,1,0:T(8,128)}, u32[]{:S(2)}) copy-start(s32[3,128,128]{2,1,0:T(8,128)} %param.13) | copy-start | bytes 589828
  6.5 304.9 %all-gather.3.cloned.1.call-start = ((), (), s32[]{:S(2)}) async-start(), calls=%async_computation.2 | async-start | bytes 2129920 | tf_op jit(solution)/shard_map/all_gather | solution.py:63
  16.1 589.9 %all-gather.5.cloned.1.call-start = ((), (), s32[]{:S(2)}) async-start(), calls=%async_computation.3 | async-start | bytes 2129920 | tf_op jit(solution)/shard_map/all_gather | solution.py:64
  606.1 3.3 copy-start.6
  626.1 5.9 copy-start.2
  632.0 1.6 copy-start.4
  654.1 5.9 copy-start.3
  660.0 1.6 copy-start.5
  664.9 0.9 copy-start.1
Sparse Core Ops, SparseCore 0:
  16.2 295.2 all-gather.2
  313.5 292.3 all-gather.4
where the time goes:
time: 673 us
  waiting for transfers between devices  574 us (85%)
  local copies, waits for them, and re-layouts  39.6 us (6%)
  other arithmetic  19.9 us (3%)
  blocking collectives  17.2 us (3%)
  between operations  14.7 us (2%)
    all_gather x1, waiting for transfers between devices, per_device(): lax.all_gather(value_rows, ('outer', 'inner'), axis=0, tiled=True)  294 us
    all_gather x1, waiting for transfers between devices, per_device(): key_piece = lax.all_gather(key_rows, ('outer', 'inner'), axis=0, tiled=True)  280 us
    reshape x2, local copies, waits for them, and re-layouts, per_device(): jnp.repeat(mask_block, block_len, axis=2) > 0  21.7 us
  transfers between devices with their start and end apart: 2, of which 2 were waited for; matrix products, arithmetic and copies ran while one was open for 1% of the time, Pallas kernels for 0%

commit v1 on v0

v1 whole, which is shorter than its diff:
```python
import jax
import jax.numpy as jnp
from jax import lax
from jax.experimental import pallas as pl
from jax.experimental.pallas import tpu as pltpu
from jax.sharding import Mesh, PartitionSpec as P

HEAD = ("x", "c")
KEYS = ("yh", "zs", "ys")
BLOCK = ("z0", "y0")
TOK = ("yh", "zs", "z0", "ys", "y0")
AXES = HEAD + TOK
SIZES = (4, 2, 2, 4, 2, 2, 2)

HD = 128
ROWS = 128
GROUP = 3
QROWS = GROUP * ROWS
BLK = 64
MASKED = -1e30
LOG2E = 1.4426950408889634
SCALE2 = HD**-0.5 * LOG2E


def attend_kernel(place_ref, q_ref, kv_ref, mask_ref, out_ref, kx_ref, vx_ref, s_ref):
    shards = kv_ref.shape[1]
    own = place_ref[0]
    lane = lax.broadcasted_iota(jnp.int32, (ROWS, HD), 1)
    row = lax.broadcasted_iota(jnp.int32, (ROWS, HD), 0)
    row_half = row // BLK
    for s in range(shards):
        rows = pl.ds(s * ROWS, ROWS)
        kx_ref[rows, :HD] = kv_ref[:, s, 0].reshape(ROWS, HD)
        vx_ref[rows, :HD] = kv_ref[:, s, 1].reshape(ROWS, HD)
        block = 2 * place_ref[8 + s] + row_half
        kx_ref[rows, HD:] = jnp.where(lane == block, 1.0, 0.0).astype(jnp.bfloat16)
        vx_ref[rows, HD:] = jnp.ones((ROWS, HD), jnp.bfloat16)

    def one_shard(j, carry):
        shard = place_ref[1 + j]
        biases = []
        for g in range(GROUP):
            for half in range(2):
                mask = mask_ref[g, pl.ds(2 * shard + half, 1), :]
                bias = jnp.where(mask > 0, 0.0, MASKED)
                biases.append(jnp.broadcast_to(bias, (BLK, HD)).astype(jnp.bfloat16))
        qx = jnp.concatenate([q_ref[j].reshape(QROWS, HD), jnp.concatenate(biases, axis=0)], axis=1)
        s_ref[...] = lax.dot_general(
            qx, kx_ref[...], (((1,), (1,)), ((), ())), preferred_element_type=jnp.float32
        )

        @pl.when(j == 0)
        def _():
            cols = pl.ds(pl.multiple_of(own * ROWS, ROWS), ROWS)
            for g in range(GROUP):
                rows = pl.ds(g * ROWS, ROWS)
                s_ref[rows, cols] = jnp.where(lane <= row, s_ref[rows, cols], MASKED)

        stats = []
        for g in range(GROUP):
            rows = pl.ds(g * ROWS, ROWS)
            scores = s_ref[rows, :]
            highest = jnp.max(scores, axis=1, keepdims=True)
            weights = jnp.exp2((scores - highest) * SCALE2).astype(jnp.bfloat16)
            both = jnp.dot(weights, vx_ref[...], preferred_element_type=jnp.float32)
            denominator = both[:, HD:]
            out_ref[j, rows, :] = (both[:, :HD] / denominator).astype(jnp.bfloat16)
            stats.append(highest * SCALE2 + jnp.log2(denominator))
        which = lane % GROUP
        level = jnp.where(which == 0, stats[0], jnp.where(which == 1, stats[1], stats[2]))
        high = level.astype(jnp.bfloat16).astype(jnp.float32)
        rest = level - high
        middle = rest.astype(jnp.bfloat16).astype(jnp.float32)
        parts = jnp.where(lane < GROUP, high, jnp.where(lane < 2 * GROUP, middle, rest - middle))
        out_ref[j, pl.ds(QROWS, 16), :] = parts.T[:16].astype(jnp.bfloat16)
        return carry

    lax.fori_loop(0, q_ref.shape[0], one_shard, 0)


def combine_kernel(p_ref, out_ref):
    parts = p_ref.shape[0]
    levels = []
    for i in range(parts):
        st = p_ref[i, pl.ds(QROWS, 16), :].astype(jnp.float32)
        levels.append(st[0:GROUP] + st[GROUP : 2 * GROUP] + st[2 * GROUP : 3 * GROUP])
    top = levels[0]
    for i in range(1, parts):
        top = jnp.maximum(top, levels[i])
    shares = [jnp.exp2(level - top) for level in levels]
    total = shares[0]
    for i in range(1, parts):
        total = total + shares[i]
    shares = [share / total for share in shares]
    pad = jnp.zeros((HD - parts * GROUP, HD), jnp.float32)
    columns = jnp.concatenate(shares + [pad], axis=0).T
    for g in range(GROUP):
        acc = None
        for i in range(parts):
            c = i * GROUP + g
            term = p_ref[i, pl.ds(g * ROWS, ROWS), :].astype(jnp.float32) * columns[:, c : c + 1]
            acc = term if acc is None else acc + term
        out_ref[g] = acc.astype(jnp.bfloat16)


def swap(value, axis):
    return lax.ppermute(value, axis, [(0, 1), (1, 0)])


def per_device(queries, key_states, value_states, head_masks):
    yh, zs, z0, ys, y0 = (lax.axis_index(a) for a in TOK)
    shard_of = lambda yh, zs, z0, ys, y0: yh * 32 + zs * 8 + z0 * 4 + ys * 2 + y0

    mine = queries.transpose(1, 0, 2)
    pair = jnp.stack([mine, swap(mine, "y0")])
    other = swap(pair, "z0")
    q_all = jnp.concatenate([pair, other], axis=0)
    q_shards = [shard_of(yh, zs, z0 ^ (j >> 1), ys, y0 ^ (j & 1)) for j in range(4)]

    kv = jnp.stack([key_states[0, 0], value_states[0, 0]]).transpose(2, 0, 1, 3)
    kv = jnp.broadcast_to(kv[:, None], (8, 16, 2, 16, HD)).reshape(128, 2, 16, HD)
    kv = lax.all_to_all(kv, HEAD + KEYS, 0, 0, tiled=True).reshape(8, 16, 2, 16, HD)
    k_shards = [shard_of(i >> 3, (i >> 1) & 3, z0, i & 1, y0) for i in range(16)]
    own = yh * 8 + zs * 2 + ys

    place = jnp.stack(
        [own] + q_shards + [jnp.int32(0)] * 3 + k_shards
    ).astype(jnp.int32)
    vmem = pl.BlockSpec(memory_space=pltpu.VMEM)
    parts = pl.pallas_call(
        attend_kernel,
        out_shape=jax.ShapeDtypeStruct((4, QROWS + 16, HD), jnp.bfloat16),
        in_specs=[pl.BlockSpec(memory_space=pltpu.SMEM), vmem, vmem, vmem],
        out_specs=vmem,
        scratch_shapes=[
            pltpu.VMEM((16 * ROWS, 2 * HD), jnp.bfloat16),
            pltpu.VMEM((16 * ROWS, 2 * HD), jnp.bfloat16),
            pltpu.VMEM((QROWS, 16 * ROWS), jnp.float32),
        ],
        compiler_params=pltpu.CompilerParams(vmem_limit_bytes=32 * 2**20),
        name="attend",
    )(place, q_all, kv, head_masks)

    got = [parts[0]] + [
        lax.ppermute(parts[j], BLOCK, [(i, i ^ j) for i in range(4)]) for j in (3, 2, 1)
    ]
    got = jnp.stack(got)
    out = pl.pallas_call(
        combine_kernel,
        out_shape=jax.ShapeDtypeStruct((GROUP, ROWS, HD), jnp.bfloat16),
        in_specs=[vmem],
        out_specs=vmem,
        compiler_params=pltpu.CompilerParams(vmem_limit_bytes=16 * 2**20),
        name="combine",
    )(got)
    return out.transpose(1, 0, 2)


def solution(mesh):
    fine = Mesh(mesh.devices.reshape(SIZES), AXES)
    return jax.shard_map(
        per_device,
        mesh=fine,
        in_specs=(P(TOK, HEAD, None), P(TOK, HEAD), P(TOK, HEAD), P(HEAD)),
        out_specs=P(TOK, HEAD, None),
        check_vma=False,
    )
```

time: 673 us -> 79.4 us (0.12)
  the two profiles are of different devices: /device:TPU:210 before, /device:TPU:8 now
where the time goes in v1:
time: 79.4 us; the launch traced here: 79.1 us
  starting transfers between devices  37.1 us (47%)
  waiting for transfers between devices  31.3 us (39%)
  Pallas kernels  8.21 us (10%)
  local copies, waits for them, and re-layouts  1.29 us (2%)
  other arithmetic  0.89 us (1%)
    ppermute x2, waiting for transfers between devices, swap(): return lax.ppermute(value, axis, [(0, 1), (1, 0)])  26.3 us
    all_to_all x1, starting transfers between devices, per_device(): lax.all_to_all(kv, HEAD + KEYS, 0, 0, tiled=True).reshape(8, 16, 2, 16, HD)  19.5 us
    ppermute x3, starting transfers between devices, per_device(): lax.ppermute(parts[j], BLOCK, [(i, i ^ j) for i in range(4)])  11 us
    pallas_call x1, Pallas kernels, per_device(): pl.pallas_call(attend_kernel, out_shape=jax.ShapeDtypeStruct((4, QROWS +...  7.14 us
    ppermute x2, starting transfers between devices, swap(): return lax.ppermute(value, axis, [(0, 1), (1, 0)])  6.64 us
    ppermute x3, waiting for transfers between devices, per_device(): lax.ppermute(parts[j], BLOCK, [(i, i ^ j) for i in range(4)])  5.06 us
  transfers between devices with their start and end apart: 6, of which 4 were waited for; matrix products, arithmetic and copies ran while one was open for 0% of the time, Pallas kernels for 0%

profile of v1, /device:TPU:8, one launch (start us, length us, event | category | flops | bytes accessed | tf_op | source)
XLA Modules:
  0.0 79.1 jit_solution(13196246949263430797)
XLA Ops:
  0.0 0.8 maximum_bitcast_fusion
  0.8 1.1 %broadcast_in_dim.2 = bf16[8,16,2,16,128]{4,3,2,1,0:T(8,128)(2,1)} broadcast(bf16[8,2,16,128]{3,2,1,0:T(8,128)(2,1)S(1)} %copy.5), dimensions={0,2,3,4} | broadcast | bytes 1114112 | tf_op jit(solution)/shard_map/broadcast_in_dim | solution.py:121
  1.9 0.0 copy-start.1
  1.9 19.5 %all-to-all-start = ((bf16[128,2,16,128]{3,2,1,0:T(8,128)(2,1)}), bf16[128,2,16,128]{3,2,1,0:T(8,128)(2,1)S(1)}, u32[]{:S(2)}, u32[]{:S(2)}) async-start(bf16[128,2,16,128]{3,2,1,0:T(8,128)(2,1)} %bitcast.28), calls=%async_computation | async-start | bytes 2097152 | tf_op jit(solution)/shard_map/all_to_all | solution.py:122
  21.4 0.0 copy-done.1
  21.4 3.3 %collective-permute-start = (bf16[3,128,128]{2,1,0:T(8,128)(2,1)S(1)}, bf16[3,128,128]{2,1,0:T(8,128)(2,1)S(1)}, u32[]{:S(2)}, u32[]{:S(2)}) collective-permute-start(bf16[3,128,128]{2,1,0:T(8,128)(2,1)S(1)} %bitcast.42), channel_id=1, source_target_pairs={{0,1},{1,0},{2,3},{3,2},{4,5},{5,4},{6,7},{7,6},{8,9},{9,8},{10,11... | collective-permute-start | bytes 294920 | tf_op jit(solution)/shard_map/ppermute | solution.py:107
  24.7 22.3 %collective-permute-done = bf16[3,128,128]{2,1,0:T(8,128)(2,1)S(1)} collective-permute-done((bf16[3,128,128]{2,1,0:T(8,128)(2,1)S(1)}, bf16[3,128,128]{2,1,0:T(8,128)(2,1)S(1)}, u32[]{:S(2)}, u32[]{:S(2)}) %collective-permute-start) | collective-permute-done | bytes 98336 | tf_op jit(solution)/shard_map/ppermute | solution.py:107
  47.0 3.4 %collective-permute-start.1 = (bf16[2,3,128,128]{3,2,1,0:T(8,128)(2,1)S(1)}, bf16[2,3,128,128]{3,2,1,0:T(8,128)(2,1)S(1)}, u32[]{:S(2)}, u32[]{:S(2)}) collective-permute-start(bf16[2,3,128,128]{3,2,1,0:T(8,128)(2,1)S(1)} %pad_maximum_fusion.2), channel_id=1, source_target_pairs={{0,4},{4,0},{1,5},{5,1},{2,6},{6,2},{3,7},{7,3},{8,12},{12,8},{9,1... | collective-permute-start | bytes 589832 | tf_op jit(solution)/shard_map/ppermute | solution.py:107
  50.5 0.1 stack.111.place_ref
  50.6 0.0 copy-start
  50.6 3.9 %collective-permute-done.1 = bf16[2,3,128,128]{3,2,1,0:T(8,128)(2,1)S(1)} collective-permute-done((bf16[2,3,128,128]{3,2,1,0:T(8,128)(2,1)S(1)}, bf16[2,3,128,128]{3,2,1,0:T(8,128)(2,1)S(1)}, u32[]{:S(2)}, u32[]{:S(2)}) %collective-permute-start.1) | collective-permute-done | bytes 196640 | tf_op jit(solution)/shard_map/ppermute | solution.py:107
  54.6 0.0 all-to-all-done
  54.6 0.0 copy-done
  54.7 7.1 %attend.1 = bf16[4,400,128]{2,1,0:T(8,128)(2,1)S(1)} custom-call(s32[24]{0:T(128)S(1)} %stack.111.place_ref, bf16[4,3,128,128]{3,2,1,0:T(8,128)(2,1)S(1)} %pad_maximum_fusion.1.q_ref, bf16[8,16,2,16,128]{4,3,2,1,0:T(8,128)(2,1)S(1)} %bitcast.41, s32[3,128,128]{2,1,0:T(8,128)S(1)} %copy-done), custom_call_target="tpu_custom_call" | custom-call | tf_op jit(solution)/shard_map/attend/pallas_call | solution.py:130
  61.8 5.7 %collective-permute-start.4 = (bf16[400,128]{1,0:T(8,128)(2,1)S(1)}, bf16[400,128]{1,0:T(8,128)(2,1)S(1)}, u32[]{:S(2)}, u32[]{:S(2)}) collective-permute-start(bf16[400,128]{1,0:T(8,128)(2,1)S(1)} %get-tuple-element.6), channel_id=1, source_target_pairs={{0,1},{1,0},{4,5},{5,4},{2,3},{3,2},{6,7},{7,6},{8,9},{9,8},{12,13... | collective-permute-start | bytes 307208 | tf_op jit(solution)/shard_map/ppermute | solution.py:145
  67.5 2.9 %collective-permute-start.3 = (bf16[400,128]{1,0:T(8,128)(2,1)S(1)}, bf16[400,128]{1,0:T(8,128)(2,1)S(1)}, u32[]{:S(2)}, u32[]{:S(2)}) collective-permute-start(bf16[400,128]{1,0:T(8,128)(2,1)S(1)} %get-tuple-element.7), channel_id=1, source_target_pairs={{0,4},{1,5},{4,0},{5,1},{2,6},{3,7},{6,2},{7,3},{8,12},{9,13},{12,... | collective-permute-start | bytes 307208 | tf_op jit(solution)/shard_map/ppermute | solution.py:145
  70.5 2.4 %collective-permute-start.2 = (bf16[400,128]{1,0:T(8,128)(2,1)S(1)}, bf16[400,128]{1,0:T(8,128)(2,1)S(1)}, u32[]{:S(2)}, u32[]{:S(2)}) collective-permute-start(bf16[400,128]{1,0:T(8,128)(2,1)S(1)} %get-tuple-element.8), channel_id=1, source_target_pairs={{0,5},{1,4},{4,1},{5,0},{2,7},{3,6},{6,3},{7,2},{8,13},{9,12},{12,... | collective-permute-start | bytes 307208 | tf_op jit(solution)/shard_map/ppermute | solution.py:145
  72.9 0.0 collective-permute-done.4
  72.9 1.2 %collective-permute-done.3 = bf16[400,128]{1,0:T(8,128)(2,1)S(1)} collective-permute-done((bf16[400,128]{1,0:T(8,128)(2,1)S(1)}, bf16[400,128]{1,0:T(8,128)(2,1)S(1)}, u32[]{:S(2)}, u32[]{:S(2)}) %collective-permute-start.3) | collective-permute-done | bytes 102432 | tf_op jit(solution)/shard_map/ppermute | solution.py:145
  74.1 3.8 %collective-permute-done.2 = bf16[400,128]{1,0:T(8,128)(2,1)S(1)} collective-permute-done((bf16[400,128]{1,0:T(8,128)(2,1)S(1)}, bf16[400,128]{1,0:T(8,128)(2,1)S(1)}, u32[]{:S(2)}, u32[]{:S(2)}) %collective-permute-start.2) | collective-permute-done | bytes 102432 | tf_op jit(solution)/shard_map/ppermute | solution.py:145
  77.9 0.1 pad_maximum_fusion.p_ref
  78.0 1.1 %combine.1 = bf16[3,128,128]{2,1,0:T(8,128)(2,1)} custom-call(bf16[4,400,128]{2,1,0:T(8,128)(2,1)S(1)} %pad_maximum_fusion.p_ref), custom_call_target="tpu_custom_call" | custom-call | tf_op jit(solution)/shard_map/combine/pallas_call | solution.py:148
  (5 shorter events, 0.1 us)
Async XLA Ops:
  1.9 19.5 %copy-start.1 = (bf16[128,3,128]{2,0,1:T(8,128)(2,1)S(1)}, bf16[128,3,128]{2,0,1:T(8,128)(2,1)}, u32[]{:S(2)}) copy-start(bf16[128,3,128]{2,0,1:T(8,128)(2,1)} %param.4) | copy-start | bytes 294916
  1.9 52.7 %all-to-all-start = ((bf16[128,2,16,128]{3,2,1,0:T(8,128)(2,1)}), bf16[128,2,16,128]{3,2,1,0:T(8,128)(2,1)S(1)}, u32[]{:S(2)}, u32[]{:S(2)}) async-start(bf16[128,2,16,128]{3,2,1,0:T(8,128)(2,1)} %bitcast.28), calls=%async_computation | async-start | bytes 2097152 | tf_op jit(solution)/shard_map/all_to_all | solution.py:122
  21.4 25.6 %collective-permute-start = (bf16[3,128,128]{2,1,0:T(8,128)(2,1)S(1)}, bf16[3,128,128]{2,1,0:T(8,128)(2,1)S(1)}, u32[]{:S(2)}, u32[]{:S(2)}) collective-permute-start(bf16[3,128,128]{2,1,0:T(8,128)(2,1)S(1)} %bitcast.42), channel_id=1, source_target_pairs={{0,1},{1,0},{2,3},{3,2},{4,5},{5,4},{6,7},{7,6},{8,9},{9,8},{10,11... | collective-permute-start | bytes 294920 | tf_op jit(solution)/shard_map/ppermute | solution.py:107
  47.0 7.6 %collective-permute-start.1 = (bf16[2,3,128,128]{3,2,1,0:T(8,128)(2,1)S(1)}, bf16[2,3,128,128]{3,2,1,0:T(8,128)(2,1)S(1)}, u32[]{:S(2)}, u32[]{:S(2)}) collective-permute-start(bf16[2,3,128,128]{3,2,1,0:T(8,128)(2,1)S(1)} %pad_maximum_fusion.2), channel_id=1, source_target_pairs={{0,4},{4,0},{1,5},{5,1},{2,6},{6,2},{3,7},{7,3},{8,12},{12,8},{9,1... | collective-permute-start | bytes 589832 | tf_op jit(solution)/shard_map/ppermute | solution.py:107
  50.6 4.0 %copy-start = (s32[3,128,128]{2,1,0:T(8,128)S(1)}, s32[3,128,128]{2,1,0:T(8,128)}, u32[]{:S(2)}) copy-start(s32[3,128,128]{2,1,0:T(8,128)} %mask_ref.1) | copy-start | bytes 589828
  61.8 11.0 %collective-permute-start.4 = (bf16[400,128]{1,0:T(8,128)(2,1)S(1)}, bf16[400,128]{1,0:T(8,128)(2,1)S(1)}, u32[]{:S(2)}, u32[]{:S(2)}) collective-permute-start(bf16[400,128]{1,0:T(8,128)(2,1)S(1)} %get-tuple-element.6), channel_id=1, source_target_pairs={{0,1},{1,0},{4,5},{5,4},{2,3},{3,2},{6,7},{7,6},{8,9},{9,8},{12,13... | collective-permute-start | bytes 307208 | tf_op jit(solution)/shard_map/ppermute | solution.py:145
  67.5 6.6 %collective-permute-start.3 = (bf16[400,128]{1,0:T(8,128)(2,1)S(1)}, bf16[400,128]{1,0:T(8,128)(2,1)S(1)}, u32[]{:S(2)}, u32[]{:S(2)}) collective-permute-start(bf16[400,128]{1,0:T(8,128)(2,1)S(1)} %get-tuple-element.7), channel_id=1, source_target_pairs={{0,4},{1,5},{4,0},{5,1},{2,6},{3,7},{6,2},{7,3},{8,12},{9,13},{12,... | collective-permute-start | bytes 307208 | tf_op jit(solution)/shard_map/ppermute | solution.py:145
  70.5 7.5 %collective-permute-start.2 = (bf16[400,128]{1,0:T(8,128)(2,1)S(1)}, bf16[400,128]{1,0:T(8,128)(2,1)S(1)}, u32[]{:S(2)}, u32[]{:S(2)}) collective-permute-start(bf16[400,128]{1,0:T(8,128)(2,1)S(1)} %get-tuple-element.8), channel_id=1, source_target_pairs={{0,5},{1,4},{4,1},{5,0},{2,7},{3,6},{6,3},{7,2},{8,13},{9,12},{12,... | collective-permute-start | bytes 307208 | tf_op jit(solution)/shard_map/ppermute | solution.py:145

commit v2 on v1

v2 whole, which is shorter than its diff:
```python
import functools

import jax
import jax.numpy as jnp
from jax import lax
from jax.experimental import pallas as pl
from jax.experimental.pallas import tpu as pltpu
from jax.sharding import Mesh, PartitionSpec as P

HEAD = ("x", "c")
TOK = ("yh", "zs", "z0", "ys", "y0")
BLOCK = ("z0", "y0")
AXES = HEAD + TOK
PLANE = ("c",) + TOK
SIZES = (4, 2, 2, 4, 2, 2, 2)

HD = 128
ROWS = 128
GROUP = 3
QROWS = GROUP * ROWS
STAT = 16
BLK = 64
FAR = 4
MASKED = -1e30
LOG2E = 1.4426950408889634
SCALE2 = HD**-0.5 * LOG2E


def plane_index(c, y, z):
    return c * 64 + (y >> 2) * 32 + z * 4 + (y & 3)


def plane_places():
    return [(c, y, z) for c in range(2) for y in range(8) for z in range(8)]


def second_axis_shift(r):
    pairs = []
    for c, y, z in plane_places():
        to = ((y + 2 * r) % 8, z) if c == 0 else (y, (z + 2 * r) % 8)
        pairs.append((plane_index(c, y, z), plane_index(c, *to)))
    return pairs


def first_axis_groups():
    groups = {}
    for x in range(4):
        for c, y, z in plane_places():
            key = (c, y, z & 1) if c == 0 else (c, y & 1, z)
            groups.setdefault(key, []).append(x * 128 + plane_index(c, y, z))
    return list(groups.values())


def shard_of(y, z):
    return (y >> 2) * 32 + z * 4 + (y & 3)


def attend_kernel(first, last, chunks, place_ref, qa_ref, qb_ref, mask_ref, *refs):
    kv_refs, refs = refs[:chunks], refs[chunks:]
    if not first:
        acc_in, top_in, den_in, refs = refs[0], refs[1], refs[2], refs[3:]
    if last:
        out_ref, refs = refs[0], refs[1:]
    else:
        acc_out, top_out, den_out, refs = refs[0], refs[1], refs[2], refs[3:]
    qx_ref, kx_ref, vx_ref, s_ref = refs
    base = 8 + (0 if first else (4 - chunks) * FAR)
    lane = lax.broadcasted_iota(jnp.int32, (ROWS, HD), 1)
    row = lax.broadcasted_iota(jnp.int32, (ROWS, HD), 0)
    row_half = row // BLK
    for n, kv_ref in enumerate(kv_refs):
        for k in range(FAR):
            s = n * FAR + k
            rows = pl.ds(s * ROWS, ROWS)
            kx_ref[:HD, rows] = kv_ref[:, k, :, 0].reshape(ROWS, HD).T
            vx_ref[rows, :HD] = kv_ref[:, k, :, 1].reshape(ROWS, HD)
            block = 2 * place_ref[base + s] + lane // BLK
            kx_ref[HD:, rows] = jnp.where(row == block, 1.0, 0.0).astype(jnp.bfloat16)
            vx_ref[rows, HD:] = jnp.ones((ROWS, HD), jnp.bfloat16)
    for j in range(4):
        src = (qa_ref, qb_ref)[j >> 1]
        shard = place_ref[1 + j]
        qx_ref[j, :, :HD] = src[j & 1].reshape(QROWS, HD)
        for g in range(GROUP):
            for half in range(2):
                bias = jnp.where(mask_ref[g, pl.ds(2 * shard + half, 1), :] > 0, 0.0, MASKED)
                rows = pl.ds(g * ROWS + half * BLK, BLK)
                qx_ref[j, rows, HD:] = jnp.broadcast_to(bias, (BLK, HD)).astype(jnp.bfloat16)

    def one_shard(j, carry):
        s_ref[j] = jnp.dot(qx_ref[j], kx_ref[...], preferred_element_type=jnp.float32)
        if first and j == 0:
            cols = pl.ds(pl.multiple_of(place_ref[0] * ROWS, ROWS), ROWS)
            for g in range(GROUP):
                rows = pl.ds(g * ROWS, ROWS)
                s_ref[j, rows, cols] = jnp.where(lane <= row, s_ref[j, rows, cols], MASKED)

        stats = []
        for g in range(GROUP):
            rows = pl.ds(g * ROWS, ROWS)
            scores = s_ref[j, rows, :]
            highest = jnp.max(scores, axis=1, keepdims=True)
            if not first:
                before = top_in[j, rows, :]
                highest = jnp.maximum(highest, before[:, :1])
            weights = jnp.exp2((scores - highest) * SCALE2).astype(jnp.bfloat16)
            both = jnp.dot(weights, vx_ref[...], preferred_element_type=jnp.float32)
            acc, denominator = both[:, :HD], both[:, HD:]
            if not first:
                keep = jnp.exp2((before - highest) * SCALE2)
                acc = acc + keep * acc_in[j, rows, :]
                denominator = denominator + keep * den_in[j, rows, :]
            if last:
                out_ref[j ^ place_ref[5], rows, :] = (acc / denominator).astype(jnp.bfloat16)
                stats.append(highest * SCALE2 + jnp.log2(denominator))
            else:
                acc_out[j, rows, :] = acc
                top_out[j, rows, :] = jnp.broadcast_to(highest, (ROWS, HD))
                den_out[j, rows, :] = denominator
        if last:
            which = lane % GROUP
            level = jnp.where(which == 0, stats[0], jnp.where(which == 1, stats[1], stats[2]))
            high = level.astype(jnp.bfloat16).astype(jnp.float32)
            rest = level - high
            middle = rest.astype(jnp.bfloat16).astype(jnp.float32)
            parts = jnp.where(lane < GROUP, high, jnp.where(lane < 2 * GROUP, middle, rest - middle))
            out_ref[j ^ place_ref[5], pl.ds(QROWS, STAT), :] = parts.T[:STAT].astype(jnp.bfloat16)
        return carry

    for j in range(4):
        one_shard(j, 0)


def attend(place, qa, qb, masks, kvs, state=None, last=False):
    chunks = len(kvs)
    vmem = pl.BlockSpec(memory_space=pltpu.VMEM)
    if last:
        outs = jax.ShapeDtypeStruct((4, QROWS + STAT, HD), jnp.bfloat16)
        out_specs = vmem
    else:
        outs = [jax.ShapeDtypeStruct((4, QROWS, HD), jnp.float32)] * 3
        out_specs = [vmem] * 3
    args = (place, qa, qb, masks, *kvs) + (tuple(state) if state is not None else ())
    keys = chunks * FAR * ROWS
    return pl.pallas_call(
        functools.partial(attend_kernel, state is None, last, chunks),
        out_shape=outs,
        in_specs=[pl.BlockSpec(memory_space=pltpu.SMEM)] + [vmem] * (len(args) - 1),
        out_specs=out_specs,
        scratch_shapes=[
            pltpu.VMEM((4, QROWS, 2 * HD), jnp.bfloat16),
            pltpu.VMEM((2 * HD, keys), jnp.bfloat16),
            pltpu.VMEM((keys, 2 * HD), jnp.bfloat16),
            pltpu.VMEM((4, QROWS, keys), jnp.float32),
        ],
        cost_estimate=pl.CostEstimate(
            flops=4 * 4 * QROWS * keys * HD * 2, bytes_accessed=2**20, transcendentals=4 * QROWS * keys
        ),
        compiler_params=pltpu.CompilerParams(vmem_limit_bytes=32 * 2**20),
        name="attend_last" if last else "attend",
    )(*args)


def combine_kernel(p_ref, out_ref):
    parts = p_ref.shape[0]
    levels = []
    for i in range(parts):
        st = p_ref[i, pl.ds(QROWS, STAT), :].astype(jnp.float32)
        levels.append(st[0:GROUP] + st[GROUP : 2 * GROUP] + st[2 * GROUP : 3 * GROUP])
    top = levels[0]
    for i in range(1, parts):
        top = jnp.maximum(top, levels[i])
    shares = [jnp.exp2(level - top) for level in levels]
    total = shares[0]
    for i in range(1, parts):
        total = total + shares[i]
    shares = [share / total for share in shares]
    pad = jnp.zeros((HD - parts * GROUP, HD), jnp.float32)
    columns = jnp.concatenate(shares + [pad], axis=0).T
    for g in range(GROUP):
        acc = None
        for i in range(parts):
            c = i * GROUP + g
            term = p_ref[i, pl.ds(g * ROWS, ROWS), :].astype(jnp.float32) * columns[:, c : c + 1]
            acc = term if acc is None else acc + term
        out_ref[g] = acc.astype(jnp.bfloat16)


def combine(parts):
    vmem = pl.BlockSpec(memory_space=pltpu.VMEM)
    return pl.pallas_call(
        combine_kernel,
        out_shape=jax.ShapeDtypeStruct((GROUP, ROWS, HD), jnp.bfloat16),
        in_specs=[vmem],
        out_specs=vmem,
        compiler_params=pltpu.CompilerParams(vmem_limit_bytes=16 * 2**20),
        name="combine",
    )(parts)


def swap(value, axis):
    return lax.ppermute(value, axis, [(0, 1), (1, 0)])


def per_device(queries, key_states, value_states, head_masks):
    c, yh, zs, z0, ys, y0 = (lax.axis_index(a) for a in PLANE)
    y, z = yh * 4 + ys * 2 + y0, zs * 2 + z0

    kv = jnp.stack([key_states[0, 0], value_states[0, 0]])
    kv = kv.transpose(2, 0, 1, 3).reshape(4, 2, 2, 16, HD)
    even, odd = kv[:, 0], kv[:, 1]
    give = jnp.where(c == 0, odd, even)
    got = swap(give, "c")
    low = jnp.where(c == 0, even, got)
    high = jnp.where(c == 0, got, odd)
    kv = jnp.stack([low, high], axis=1)
    kv = jnp.broadcast_to(kv[:, None], (4, FAR, 2, 2, 16, HD)).reshape(4 * FAR, 2, 2, 16, HD)
    own = lax.all_to_all(kv, AXES, 0, 0, axis_index_groups=first_axis_groups(), tiled=True)

    mine = queries.transpose(1, 0, 2)
    qa = jnp.stack([mine, swap(mine, "y0")])
    qb = swap(qa, "z0")

    down = lax.ppermute(own, PLANE, second_axis_shift(3))
    up = lax.ppermute(own, PLANE, second_axis_shift(1))
    far = lax.ppermute(down, PLANE, second_axis_shift(3))
    shape = (4, FAR, 2, 2, 16, HD)
    chunk = {r: a.reshape(shape) for r, a in ((0, own), (1, up), (3, down), (2, far))}

    q_shards = [shard_of(y ^ (j & 1), z ^ (j >> 1)) for j in range(4)]
    k_shards = []
    for r in (0, 1, 3, 2):
        for k in range(FAR):
            yk = jnp.where(c == 0, (y - 2 * r) & 7, 2 * k + y0)
            zk = jnp.where(c == 0, 2 * k + z0, (z - 2 * r) & 7)
            k_shards.append(shard_of(yk, zk))
    own_place = jnp.where(c == 0, z >> 1, y >> 1)
    me = z0 * 2 + y0
    zero = jnp.int32(0)
    place = jnp.stack([own_place, *q_shards, me, zero, zero, *k_shards]).astype(jnp.int32)

    state = attend(place, qa, qb, head_masks, [chunk[0], chunk[1], chunk[3]])
    parts = attend(place, qa, qb, head_masks, [chunk[2]], state, last=True)
    parts = lax.all_to_all(parts, BLOCK, 0, 0, tiled=True)
    return combine(parts).transpose(1, 0, 2)


def solution(mesh):
    fine = Mesh(mesh.devices.reshape(SIZES), AXES)
    return jax.shard_map(
        per_device,
        mesh=fine,
        in_specs=(P(TOK, HEAD, None), P(TOK, HEAD), P(TOK, HEAD), P(HEAD)),
        out_specs=P(TOK, HEAD, None),
        check_vma=False,
    )
```

time: 79.4 us -> 69.6 us (0.88)
  the two profiles are of different devices: /device:TPU:8 before, /device:TPU:48 now
where the time goes in v2:
time: 69.6 us; the launch traced here: 69.1 us
  starting transfers between devices  31.1 us (45%)
  waiting for transfers between devices  17.9 us (26%)
  blocking collectives  9.19 us (13%)
  Pallas kernels  8.7 us (12%)
  local copies, waits for them, and re-layouts  1.67 us (2%)
    all_to_all x1, starting transfers between devices, per_device(): lax.all_to_all(kv, AXES, 0, 0, axis_index_groups=first_axis_groups(), til...  13 us
    all_to_all x1, waiting for transfers between devices, per_device(): lax.all_to_all(kv, AXES, 0, 0, axis_index_groups=first_axis_groups(), til...  9.72 us
    all_to_all x1, blocking collectives, per_device(): parts = lax.all_to_all(parts, BLOCK, 0, 0, tiled=True)  9.19 us
    pallas_call x2, Pallas kernels, attend(): pl.pallas_call(functools.partial(attend_kernel, state is None, last, chun...  7.63 us
    ppermute x3, starting transfers between devices, swap(): return lax.ppermute(value, axis, [(0, 1), (1, 0)])  7.36 us
    ppermute x3, waiting for transfers between devices, swap(): return lax.ppermute(value, axis, [(0, 1), (1, 0)])  4.92 us
    ppermute x1, starting transfers between devices, per_device(): down = lax.ppermute(own, PLANE, second_axis_shift(3))  4.03 us
    ppermute x1, starting transfers between devices, per_device(): up = lax.ppermute(own, PLANE, second_axis_shift(1))  3.91 us
  transfers between devices with their start and end apart: 7, of which 5 were waited for; matrix products, arithmetic and copies ran while one was open for 0% of the time, Pallas kernels for 6%

profile of v2, /device:TPU:48, one launch (start us, length us, event | category | flops | bytes accessed | tf_op | source)
XLA Modules:
  0.0 69.1 jit_solution(14525674430375212370)
XLA Ops:
  0.0 0.8 %copy_bitcast_fusion = (bf16[1,16,8,128]{3,1,0,2:T(8,128)(2,1)S(1)}, bf16[1,16,8,128]{3,1,0,2:T(8,128)(2,1)S(1)}) fusion(bf16[1,1,16,8,128]{4,3,2,1,0:T(8,128)(2,1)} %param.6, bf16[1,1,16,8,128]{4,3,2,1,0:T(8,128)(2,1)} %param.5), kind=kLoop, calls=%fused_computation.5 | loop fusion | bytes 131072 | tf_op jit(solution)/shard_map/stack;squeeze | solution.py:209
  0.8 1.9 %collective-permute-start.2 = (bf16[4,2,16,128]{3,2,1,0:T(8,128)(2,1)S(1)}, bf16[4,2,16,128]{3,2,1,0:T(8,128)(2,1)S(1)}, u32[]{:S(2)}, u32[]{:S(2)}) collective-permute-start(bf16[4,2,16,128]{3,2,1,0:T(8,128)(2,1)S(1)} %broadcast_select_fusion), channel_id=1, source_target_pairs={{0,64},{64,0},{1,65},{65,1},{2,66},{66,2},{3,67},{67,3},{4,68},{68... | collective-permute-start | bytes 98312 | tf_op jit(solution)/shard_map/ppermute | solution.py:202
  2.8 1.2 %collective-permute-done.2 = bf16[4,2,16,128]{3,2,1,0:T(8,128)(2,1)S(1)} collective-permute-done((bf16[4,2,16,128]{3,2,1,0:T(8,128)(2,1)S(1)}, bf16[4,2,16,128]{3,2,1,0:T(8,128)(2,1)S(1)}, u32[]{:S(2)}, u32[]{:S(2)}) %collective-permute-start.2) | collective-permute-done | bytes 32800 | tf_op jit(solution)/shard_map/ppermute | solution.py:202
  4.0 0.8 %broadcast_in_dim.2 = bf16[4,4,2,2,16,128]{5,4,3,2,1,0:T(8,128)(2,1)} broadcast(bf16[4,2,2,16,128]{4,3,2,1,0:T(8,128)(2,1)S(1)} %copy.10), dimensions={0,2,3,4,5} | broadcast | bytes 327680 | tf_op jit(solution)/shard_map/broadcast_in_dim | solution.py:217
  4.7 0.0 copy-start.1
  4.7 13.0 %all-to-all-start = ((bf16[16,2,2,16,128]{4,3,2,1,0:T(8,128)(2,1)}), bf16[16,2,2,16,128]{4,3,2,1,0:T(8,128)(2,1)S(1)}, u32[]{:S(2)}, u32[]{:S(2)}) async-start(bf16[16,2,2,16,128]{4,3,2,1,0:T(8,128)(2,1)} %bitcast.34), calls=%async_computation | async-start | bytes 524288 | tf_op jit(solution)/shard_map/all_to_all | solution.py:218
  17.7 0.0 copy-done.1
  17.7 2.6 %collective-permute-start = (bf16[3,128,128]{2,1,0:T(8,128)(2,1)S(1)}, bf16[3,128,128]{2,1,0:T(8,128)(2,1)S(1)}, u32[]{:S(2)}, u32[]{:S(2)}) collective-permute-start(bf16[3,128,128]{2,1,0:T(8,128)(2,1)S(1)} %bitcast.61), channel_id=1, source_target_pairs={{0,1},{1,0},{2,3},{3,2},{4,5},{5,4},{6,7},{7,6},{8,9},{9,8},{10,11... | collective-permute-start | bytes 294920 | tf_op jit(solution)/shard_map/ppermute | solution.py:202
  20.3 9.7 %all-to-all-done = bf16[16,2,2,16,128]{4,3,2,1,0:T(8,128)(2,1)S(1)} async-done(((bf16[16,2,2,16,128]{4,3,2,1,0:T(8,128)(2,1)}), bf16[16,2,2,16,128]{4,3,2,1,0:T(8,128)(2,1)S(1)}, u32[]{:S(2)}, u32[]{:S(2)}) %all-to-all-start) | async-done | bytes 262176 | tf_op jit(solution)/shard_map/all_to_all | solution.py:218
  30.1 4.0 %collective-permute-start.3 = (bf16[16,2,2,16,128]{4,3,2,1,0:T(8,128)(2,1)S(1)}, bf16[16,2,2,16,128]{4,3,2,1,0:T(8,128)(2,1)S(1)}, u32[]{:S(2)}, u32[]{:S(2)}) collective-permute-start(bf16[16,2,2,16,128]{4,3,2,1,0:T(8,128)(2,1)S(1)} %all-to-all-done), channel_id=1, source_target_pairs={{0,34},{4,38},{8,42},{12,46},{16,50},{20,54},{24,58},{28,62},{1,35... | collective-permute-start | bytes 786440 | tf_op jit(solution)/shard_map/ppermute | solution.py:224
  34.1 3.9 %collective-permute-start.5 = (bf16[16,2,2,16,128]{4,3,2,1,0:T(8,128)(2,1)S(1)}, bf16[16,2,2,16,128]{4,3,2,1,0:T(8,128)(2,1)S(1)}, u32[]{:S(2)}, u32[]{:S(2)}) collective-permute-start(bf16[16,2,2,16,128]{4,3,2,1,0:T(8,128)(2,1)S(1)} %all-to-all-done), channel_id=1, source_target_pairs={{0,2},{4,6},{8,10},{12,14},{16,18},{20,22},{24,26},{28,30},{1,3},{... | collective-permute-start | bytes 786440 | tf_op jit(solution)/shard_map/ppermute | solution.py:225
  38.0 0.0 collective-permute-done
  38.1 2.9 %collective-permute-start.1 = (bf16[2,3,128,128]{3,2,1,0:T(8,128)(2,1)S(1)}, bf16[2,3,128,128]{3,2,1,0:T(8,128)(2,1)S(1)}, u32[]{:S(2)}, u32[]{:S(2)}) collective-permute-start(bf16[2,3,128,128]{3,2,1,0:T(8,128)(2,1)S(1)} %pad_maximum_fusion.qa_ref), channel_id=1, source_target_pairs={{0,4},{4,0},{1,5},{5,1},{2,6},{6,2},{3,7},{7,3},{8,12},{12,8},{9,1... | collective-permute-start | bytes 589832 | tf_op jit(solution)/shard_map/ppermute | solution.py:202
  40.9 2.3 %collective-permute-done.3 = bf16[16,2,2,16,128]{4,3,2,1,0:T(8,128)(2,1)S(1)} collective-permute-done((bf16[16,2,2,16,128]{4,3,2,1,0:T(8,128)(2,1)S(1)}, bf16[16,2,2,16,128]{4,3,2,1,0:T(8,128)(2,1)S(1)}, u32[]{:S(2)}, u32[]{:S(2)}) %collective-permute-start.3) | collective-permute-done | bytes 262176 | tf_op jit(solution)/shard_map/ppermute | solution.py:224
  43.2 2.8 %collective-permute-start.4 = (bf16[16,2,2,16,128]{4,3,2,1,0:T(8,128)(2,1)S(1)}, bf16[16,2,2,16,128]{4,3,2,1,0:T(8,128)(2,1)S(1)}, u32[]{:S(2)}, u32[]{:S(2)}) collective-permute-start(bf16[16,2,2,16,128]{4,3,2,1,0:T(8,128)(2,1)S(1)} %collective-permute-done.3), channel_id=1, source_target_pairs={{0,34},{4,38},{8,42},{12,46},{16,50},{20,54},{24,58},{28,62},{1,35... | collective-permute-start | bytes 786440 | tf_op jit(solution)/shard_map/ppermute | solution.py:226
  46.1 0.0 copy-start
  46.4 0.1 stack.112.place_ref
  46.5 3.7 %collective-permute-done.1.qb_ref = bf16[2,3,128,128]{3,2,1,0:T(8,128)(2,1)S(1)} collective-permute-done((bf16[2,3,128,128]{3,2,1,0:T(8,128)(2,1)S(1)}, bf16[2,3,128,128]{3,2,1,0:T(8,128)(2,1)S(1)}, u32[]{:S(2)}, u32[]{:S(2)}) %collective-permute-start.1) | collective-permute-done | bytes 196640 | tf_op jit(solution)/shard_map/ppermute | solution.py:202
  50.2 0.0 collective-permute-done.5
  50.2 0.0 copy-done
  50.2 4.4 %attend.1 = (f32[4,384,128]{2,1,0:T(8,128)S(1)}, f32[4,384,128]{2,1,0:T(8,128)S(1)}, f32[4,384,128]{2,1,0:T(8,128)S(1)}) custom-call(s32[24]{0:T(128)S(1)} %stack.112.place_ref, bf16[2,3,128,128]{3,2,1,0:T(8,128)(2,1)S(1)} %pad_maximum_fusion.qa_ref, bf16[2,3,128,128]{3,2,1,0:T(8,128)(2,1)S(1)} %collective-permute-done.1.qb_ref, s32[3,128,128]{2,1,0:T(8,128)S(1)} %copy-done, ...), custom_call_target="tpu_custom_call" | custom-call | flops 2415919104 | bytes 1048576 | tf_op jit(solution)/shard_map/attend/pallas_call | solution.py:145
  54.7 0.9 %collective-permute-done.4 = bf16[16,2,2,16,128]{4,3,2,1,0:T(8,128)(2,1)S(1)} collective-permute-done((bf16[16,2,2,16,128]{4,3,2,1,0:T(8,128)(2,1)S(1)}, bf16[16,2,2,16,128]{4,3,2,1,0:T(8,128)(2,1)S(1)}, u32[]{:S(2)}, u32[]{:S(2)}) %collective-permute-start.4) | collective-permute-done | bytes 262176 | tf_op jit(solution)/shard_map/ppermute | solution.py:226
  55.6 3.2 %attend_last.1 = bf16[4,400,128]{2,1,0:T(8,128)(2,1)S(1)} custom-call(s32[24]{0:T(128)S(1)} %stack.112.place_ref, bf16[2,3,128,128]{3,2,1,0:T(8,128)(2,1)S(1)} %pad_maximum_fusion.qa_ref, bf16[2,3,128,128]{3,2,1,0:T(8,128)(2,1)S(1)} %collective-permute-done.1.qb_ref, s32[3,128,128]{2,1,0:T(8,128)S(1)} %copy-done, ...), custom_call_target="tpu_custom_call" | custom-call | flops 805306368 | bytes 1048576 | tf_op jit(solution)/shard_map/attend_last/pallas_call | solution.py:145
  58.8 9.2 %all_to_all.10.p_ref = bf16[4,400,128]{2,1,0:T(8,128)(2,1)S(1)} all-to-all(bf16[4,400,128]{2,1,0:T(8,128)(2,1)S(1)} %attend_last.1), channel_id=1, replica_groups=mesh['x'=4,'c'=2,'yh'=2,'zs'=4,'z0'=2,'ys'=2,'y0'=2] {'z0','y0'}, dimensions={0} | all-to-all | bytes 819200 | tf_op jit(solution)/shard_map/all_to_all | solution.py:244
  68.0 1.1 %combine.1 = bf16[3,128,128]{2,1,0:T(8,128)(2,1)} custom-call(bf16[4,400,128]{2,1,0:T(8,128)(2,1)S(1)} %all_to_all.10.p_ref), custom_call_target="tpu_custom_call" | custom-call | tf_op jit(solution)/shard_map/combine/pallas_call | solution.py:191
  (7 shorter events, 0.1 us)
Async XLA Ops:
  0.8 3.1 %collective-permute-start.2 = (bf16[4,2,16,128]{3,2,1,0:T(8,128)(2,1)S(1)}, bf16[4,2,16,128]{3,2,1,0:T(8,128)(2,1)S(1)}, u32[]{:S(2)}, u32[]{:S(2)}) collective-permute-start(bf16[4,2,16,128]{3,2,1,0:T(8,128)(2,1)S(1)} %broadcast_select_fusion), channel_id=1, source_target_pairs={{0,64},{64,0},{1,65},{65,1},{2,66},{66,2},{3,67},{67,3},{4,68},{68... | collective-permute-start | bytes 98312 | tf_op jit(solution)/shard_map/ppermute | solution.py:202
  4.7 13.0 %copy-start.1 = (bf16[128,3,128]{2,0,1:T(8,128)(2,1)S(1)}, bf16[128,3,128]{2,0,1:T(8,128)(2,1)}, u32[]{:S(2)}) copy-start(bf16[128,3,128]{2,0,1:T(8,128)(2,1)} %param.4) | copy-start | bytes 294916
  4.7 25.3 %all-to-all-start = ((bf16[16,2,2,16,128]{4,3,2,1,0:T(8,128)(2,1)}), bf16[16,2,2,16,128]{4,3,2,1,0:T(8,128)(2,1)S(1)}, u32[]{:S(2)}, u32[]{:S(2)}) async-start(bf16[16,2,2,16,128]{4,3,2,1,0:T(8,128)(2,1)} %bitcast.34), calls=%async_computation | async-start | bytes 524288 | tf_op jit(solution)/shard_map/all_to_all | solution.py:218
  17.7 20.3 %collective-permute-start = (bf16[3,128,128]{2,1,0:T(8,128)(2,1)S(1)}, bf16[3,128,128]{2,1,0:T(8,128)(2,1)S(1)}, u32[]{:S(2)}, u32[]{:S(2)}) collective-permute-start(bf16[3,128,128]{2,1,0:T(8,128)(2,1)S(1)} %bitcast.61), channel_id=1, source_target_pairs={{0,1},{1,0},{2,3},{3,2},{4,5},{5,4},{6,7},{7,6},{8,9},{9,8},{10,11... | collective-permute-start | bytes 294920 | tf_op jit(solution)/shard_map/ppermute | solution.py:202
  30.1 13.2 %collective-permute-start.3 = (bf16[16,2,2,16,128]{4,3,2,1,0:T(8,128)(2,1)S(1)}, bf16[16,2,2,16,128]{4,3,2,1,0:T(8,128)(2,1)S(1)}, u32[]{:S(2)}, u32[]{:S(2)}) collective-permute-start(bf16[16,2,2,16,128]{4,3,2,1,0:T(8,128)(2,1)S(1)} %all-to-all-done), channel_id=1, source_target_pairs={{0,34},{4,38},{8,42},{12,46},{16,50},{20,54},{24,58},{28,62},{1,35... | collective-permute-start | bytes 786440 | tf_op jit(solution)/shard_map/ppermute | solution.py:224
  34.1 16.1 %collective-permute-start.5 = (bf16[16,2,2,16,128]{4,3,2,1,0:T(8,128)(2,1)S(1)}, bf16[16,2,2,16,128]{4,3,2,1,0:T(8,128)(2,1)S(1)}, u32[]{:S(2)}, u32[]{:S(2)}) collective-permute-start(bf16[16,2,2,16,128]{4,3,2,1,0:T(8,128)(2,1)S(1)} %all-to-all-done), channel_id=1, source_target_pairs={{0,2},{4,6},{8,10},{12,14},{16,18},{20,22},{24,26},{28,30},{1,3},{... | collective-permute-start | bytes 786440 | tf_op jit(solution)/shard_map/ppermute | solution.py:225
  38.1 12.2 %collective-permute-start.1 = (bf16[2,3,128,128]{3,2,1,0:T(8,128)(2,1)S(1)}, bf16[2,3,128,128]{3,2,1,0:T(8,128)(2,1)S(1)}, u32[]{:S(2)}, u32[]{:S(2)}) collective-permute-start(bf16[2,3,128,128]{3,2,1,0:T(8,128)(2,1)S(1)} %pad_maximum_fusion.qa_ref), channel_id=1, source_target_pairs={{0,4},{4,0},{1,5},{5,1},{2,6},{6,2},{3,7},{7,3},{8,12},{12,8},{9,1... | collective-permute-start | bytes 589832 | tf_op jit(solution)/shard_map/ppermute | solution.py:202
  43.2 12.4 %collective-permute-start.4 = (bf16[16,2,2,16,128]{4,3,2,1,0:T(8,128)(2,1)S(1)}, bf16[16,2,2,16,128]{4,3,2,1,0:T(8,128)(2,1)S(1)}, u32[]{:S(2)}, u32[]{:S(2)}) collective-permute-start(bf16[16,2,2,16,128]{4,3,2,1,0:T(8,128)(2,1)S(1)} %collective-permute-done.3), channel_id=1, source_target_pairs={{0,34},{4,38},{8,42},{12,46},{16,50},{20,54},{24,58},{28,62},{1,35... | collective-permute-start | bytes 786440 | tf_op jit(solution)/shard_map/ppermute | solution.py:226
  46.1 4.2 %copy-start = (s32[3,128,128]{2,1,0:T(8,128)S(1)}, s32[3,128,128]{2,1,0:T(8,128)}, u32[]{:S(2)}) copy-start(s32[3,128,128]{2,1,0:T(8,128)} %mask_ref.3) | copy-start | bytes 589828

commit v3 on v2

v3 whole, which is shorter than its diff:
```python
import functools

import jax
import jax.numpy as jnp
from jax import lax
from jax.experimental import pallas as pl
from jax.experimental.pallas import tpu as pltpu
from jax.sharding import Mesh, PartitionSpec as P

HEAD = ("x", "c")
TOK = ("yh", "zs", "z0", "ys", "y0")
BLOCK = ("z0", "y0")
AXES = HEAD + TOK
PLANE = ("c",) + TOK
SIZES = (4, 2, 2, 4, 2, 2, 2)

HD = 128
ROWS = 128
GROUP = 3
QROWS = GROUP * ROWS
STAT = 16
BLK = 64
FAR = 4
MASKED = -1e30
LOG2E = 1.4426950408889634
CHUNKS = 8
SCALE2 = HD**-0.5 * LOG2E


def plane_index(c, y, z):
    return c * 64 + (y >> 2) * 32 + z * 4 + (y & 3)


def plane_places():
    return [(c, y, z) for c in range(2) for y in range(8) for z in range(8)]


def second_axis_xor(bits):
    pairs = []
    for c, y, z in plane_places():
        to = (y ^ bits, z) if c == 0 else (y, z ^ bits)
        pairs.append((plane_index(c, y, z), plane_index(c, *to)))
    return pairs


def first_axis_groups():
    groups = {}
    for x in range(4):
        for c, y, z in plane_places():
            key = (c, y, z & 1) if c == 0 else (c, y & 1, z)
            groups.setdefault(key, []).append(x * 128 + plane_index(c, y, z))
    return list(groups.values())


def shard_of(y, z):
    return (y >> 2) * 32 + z * 4 + (y & 3)


def load_operands(base, place_ref, qa_ref, qb_ref, mask_ref, kv_refs, qx_ref, kx_ref, vx_ref):
    lane = lax.broadcasted_iota(jnp.int32, (ROWS, HD), 1)
    row = lax.broadcasted_iota(jnp.int32, (ROWS, HD), 0)
    row_half = row // BLK
    for n, kv_ref in enumerate(kv_refs):
        for k in range(FAR):
            s = n * FAR + k
            rows = pl.ds(s * ROWS, ROWS)
            kx_ref[:HD, rows] = kv_ref[:, k, :, 0].reshape(ROWS, HD).T
            vx_ref[rows, :HD] = kv_ref[:, k, :, 1].reshape(ROWS, HD)
            block = 2 * place_ref[base + s] + lane // BLK
            kx_ref[HD:, rows] = jnp.where(row == block, 1.0, 0.0).astype(jnp.bfloat16)
            vx_ref[rows, HD:] = jnp.ones((ROWS, HD), jnp.bfloat16)
    for j in range(4):
        src = (qa_ref, qb_ref)[j >> 1]
        shard = place_ref[1 + j]
        qx_ref[j, :, :HD] = src[j & 1].reshape(QROWS, HD)
        for g in range(GROUP):
            for half in range(2):
                bias = jnp.where(mask_ref[g, pl.ds(2 * shard + half, 1), :] > 0, 0.0, MASKED)
                rows = pl.ds(g * ROWS + half * BLK, BLK)
                qx_ref[j, rows, HD:] = jnp.broadcast_to(bias, (BLK, HD)).astype(jnp.bfloat16)
    return lane, row


def attend_kernel(chunks, place_ref, qa_ref, qb_ref, mask_ref, *refs):
    kv_refs, (acc_out, top_out, den_out, qx_ref, kx_ref, vx_ref, s_ref, p_ref) = refs[:chunks], refs[chunks:]
    lane, row = load_operands(CHUNKS, place_ref, qa_ref, qb_ref, mask_ref, kv_refs, qx_ref, kx_ref, vx_ref)
    tops = {}
    for j in range(4):
        s_ref[j] = jnp.dot(qx_ref[j], kx_ref[...], preferred_element_type=jnp.float32)
    cols = pl.ds(pl.multiple_of(place_ref[0] * ROWS, ROWS), ROWS)
    for g in range(GROUP):
        rows = pl.ds(g * ROWS, ROWS)
        s_ref[0, rows, cols] = jnp.where(lane <= row, s_ref[0, rows, cols], MASKED)
    for j in range(4):
        for g in range(GROUP):
            rows = pl.ds(g * ROWS, ROWS)
            tops[j, g] = jnp.max(s_ref[j, rows, :], axis=1, keepdims=True)
    for j in range(4):
        for g in range(GROUP):
            rows = pl.ds(g * ROWS, ROWS)
            p_ref[j, rows, :] = jnp.exp2((s_ref[j, rows, :] - tops[j, g]) * SCALE2).astype(jnp.bfloat16)
    for j in range(4):
        both = jnp.dot(p_ref[j], vx_ref[...], preferred_element_type=jnp.float32)
        acc_out[j] = both[:, :HD]
        den_out[j] = both[:, HD:]
        for g in range(GROUP):
            top_out[j, pl.ds(g * ROWS, ROWS), :] = jnp.broadcast_to(tops[j, g], (ROWS, HD))


def attend_last_kernel(
    place_ref, qa_ref, qb_ref, mask_ref, kv_ref, acc_in, top_in, den_in, out_ref, qx_ref, kx_ref, vx_ref, s_ref
):
    base = CHUNKS + 3 * FAR
    lane, _ = load_operands(base, place_ref, qa_ref, qb_ref, mask_ref, [kv_ref], qx_ref, kx_ref, vx_ref)
    for j in range(4):
        s_ref[j] = jnp.dot(qx_ref[j], kx_ref[...], preferred_element_type=jnp.float32)
        slot = j ^ place_ref[5]
        stats = []
        for g in range(GROUP):
            rows = pl.ds(g * ROWS, ROWS)
            scores = s_ref[j, rows, :]
            before = top_in[j, rows, :]
            highest = jnp.maximum(jnp.max(scores, axis=1, keepdims=True), before[:, :1])
            weights = jnp.exp2((scores - highest) * SCALE2).astype(jnp.bfloat16)
            both = jnp.dot(weights, vx_ref[...], preferred_element_type=jnp.float32)
            keep = jnp.exp2((before - highest) * SCALE2)
            acc = both[:, :HD] + keep * acc_in[j, rows, :]
            denominator = both[:, HD:] + keep * den_in[j, rows, :]
            out_ref[slot, rows, :] = (acc / denominator).astype(jnp.bfloat16)
            stats.append(highest * SCALE2 + jnp.log2(denominator))
        which = lane % GROUP
        level = jnp.where(which == 0, stats[0], jnp.where(which == 1, stats[1], stats[2]))
        high = level.astype(jnp.bfloat16).astype(jnp.float32)
        rest = level - high
        middle = rest.astype(jnp.bfloat16).astype(jnp.float32)
        parts = jnp.where(lane < GROUP, high, jnp.where(lane < 2 * GROUP, middle, rest - middle))
        out_ref[slot, pl.ds(QROWS, STAT), :] = parts.T[:STAT].astype(jnp.bfloat16)


def attend(place, qa, qb, masks, kvs, state=None):
    vmem = pl.BlockSpec(memory_space=pltpu.VMEM)
    keys = len(kvs) * FAR * ROWS
    scratch = [
        pltpu.VMEM((4, QROWS, 2 * HD), jnp.bfloat16),
        pltpu.VMEM((2 * HD, keys), jnp.bfloat16),
        pltpu.VMEM((keys, 2 * HD), jnp.bfloat16),
        pltpu.VMEM((4, QROWS, keys), jnp.float32),
    ]
    if state is None:
        kernel, name, state = functools.partial(attend_kernel, len(kvs)), "attend", ()
        outs = [jax.ShapeDtypeStruct((4, QROWS, HD), jnp.float32)] * 3
        scratch.append(pltpu.VMEM((4, QROWS, keys), jnp.bfloat16))
    else:
        kernel, name = attend_last_kernel, "attend_last"
        outs = jax.ShapeDtypeStruct((4, QROWS + STAT, HD), jnp.bfloat16)
    args = (place, qa, qb, masks, *kvs, *state)
    return pl.pallas_call(
        kernel,
        out_shape=outs,
        in_specs=[pl.BlockSpec(memory_space=pltpu.SMEM)] + [vmem] * (len(args) - 1),
        out_specs=[vmem] * 3 if isinstance(outs, list) else vmem,
        scratch_shapes=scratch,
        cost_estimate=pl.CostEstimate(
            flops=4 * 4 * QROWS * keys * HD * 2, bytes_accessed=2**20, transcendentals=4 * QROWS * keys
        ),
        compiler_params=pltpu.CompilerParams(vmem_limit_bytes=32 * 2**20),
        name=name,
    )(*args)


def combine_kernel(p_ref, out_ref):
    parts = p_ref.shape[0]
    levels = []
    for i in range(parts):
        st = p_ref[i, pl.ds(QROWS, STAT), :].astype(jnp.float32)
        levels.append(st[0:GROUP] + st[GROUP : 2 * GROUP] + st[2 * GROUP : 3 * GROUP])
    top = levels[0]
    for i in range(1, parts):
        top = jnp.maximum(top, levels[i])
    shares = [jnp.exp2(level - top) for level in levels]
    total = shares[0]
    for i in range(1, parts):
        total = total + shares[i]
    shares = [share / total for share in shares]
    pad = jnp.zeros((HD - parts * GROUP, HD), jnp.float32)
    columns = jnp.concatenate(shares + [pad], axis=0).T
    for g in range(GROUP):
        acc = None
        for i in range(parts):
            c = i * GROUP + g
            term = p_ref[i, pl.ds(g * ROWS, ROWS), :].astype(jnp.float32) * columns[:, c : c + 1]
            acc = term if acc is None else acc + term
        out_ref[g] = acc.astype(jnp.bfloat16)


def combine(parts):
    vmem = pl.BlockSpec(memory_space=pltpu.VMEM)
    return pl.pallas_call(
        combine_kernel,
        out_shape=jax.ShapeDtypeStruct((GROUP, ROWS, HD), jnp.bfloat16),
        in_specs=[vmem],
        out_specs=vmem,
        compiler_params=pltpu.CompilerParams(vmem_limit_bytes=16 * 2**20),
        name="combine",
    )(parts)


def swap(value, axis):
    return lax.ppermute(value, axis, [(0, 1), (1, 0)])


def per_device(queries, key_states, value_states, head_masks):
    c, yh, zs, z0, ys, y0 = (lax.axis_index(a) for a in PLANE)
    y, z = yh * 4 + ys * 2 + y0, zs * 2 + z0

    kv = jnp.stack([key_states[0, 0], value_states[0, 0]])
    kv = kv.transpose(2, 0, 1, 3).reshape(4, 2, 2, 16, HD)
    even, odd = kv[:, 0], kv[:, 1]
    give = jnp.where(c == 0, odd, even)
    got = swap(give, "c")
    low = jnp.where(c == 0, even, got)
    high = jnp.where(c == 0, got, odd)
    kv = jnp.stack([low, high], axis=1)
    kv = jnp.broadcast_to(kv[:, None], (4, FAR, 2, 2, 16, HD)).reshape(4 * FAR, 2, 2, 16, HD)
    own = lax.all_to_all(kv, AXES, 0, 0, axis_index_groups=first_axis_groups(), tiled=True)

    mine = queries.transpose(1, 0, 2)
    qa = jnp.stack([mine, swap(mine, "y0")])
    qb = swap(qa, "z0")

    low = lax.ppermute(own, PLANE, second_axis_xor(6))
    high = lax.ppermute(own, PLANE, second_axis_xor(2))
    far = lax.ppermute(low, PLANE, second_axis_xor(2))
    own, low, high, far = (a.reshape(4, FAR, 2, 2, 16, HD) for a in (own, low, high, far))

    q_shards = [shard_of(y ^ (j & 1), z ^ (j >> 1)) for j in range(4)]
    k_shards = []
    for bits in (0, 2, 6, 4):
        for k in range(FAR):
            yk = jnp.where(c == 0, y ^ bits, 2 * k + y0)
            zk = jnp.where(c == 0, 2 * k + z0, z ^ bits)
            k_shards.append(shard_of(yk, zk))
    own_place = jnp.where(c == 0, z >> 1, y >> 1)
    me = z0 * 2 + y0
    zero = jnp.int32(0)
    place = jnp.stack([own_place, *q_shards, me, zero, zero, *k_shards]).astype(jnp.int32)

    state = attend(place, qa, qb, head_masks, [own, high, low])
    parts = attend(place, qa, qb, head_masks, [far], state)
    parts = lax.all_to_all(parts, BLOCK, 0, 0, tiled=True)
    return combine(parts).transpose(1, 0, 2)


def solution(mesh):
    fine = Mesh(mesh.devices.reshape(SIZES), AXES)
    return jax.shard_map(
        per_device,
        mesh=fine,
        in_specs=(P(TOK, HEAD, None), P(TOK, HEAD), P(TOK, HEAD), P(HEAD)),
        out_specs=P(TOK, HEAD, None),
        check_vma=False,
    )
```

time: 69.6 us -> 68.2 us (0.980)
  the two profiles are of different devices: /device:TPU:48 before, /device:TPU:8 now
where the time goes in v3:
time: 68.2 us; the launch traced here: 67.7 us
  starting transfers between devices  32.1 us (47%)
  waiting for transfers between devices  16 us (23%)
  blocking collectives  9.1 us (13%)
  Pallas kernels  8.32 us (12%)
  local copies, waits for them, and re-layouts  1.67 us (2%)
    all_to_all x1, starting transfers between devices, per_device(): lax.all_to_all(kv, AXES, 0, 0, axis_index_groups=first_axis_groups(), til...  13 us
    all_to_all x1, waiting for transfers between devices, per_device(): lax.all_to_all(kv, AXES, 0, 0, axis_index_groups=first_axis_groups(), til...  9.95 us
    all_to_all x1, blocking collectives, per_device(): parts = lax.all_to_all(parts, BLOCK, 0, 0, tiled=True)  9.1 us
    pallas_call x2, Pallas kernels, attend(): pl.pallas_call(kernel, out_shape=outs, in_specs=[pl.BlockSpec(memory_spac...  7.25 us
    ppermute x3, starting transfers between devices, swap(): return lax.ppermute(value, axis, [(0, 1), (1, 0)])  7.13 us
    ppermute x1, starting transfers between devices, per_device(): low = lax.ppermute(own, PLANE, second_axis_xor(6))  5.25 us
    ppermute x3, waiting for transfers between devices, swap(): return lax.ppermute(value, axis, [(0, 1), (1, 0)])  4.99 us
    ppermute x1, starting transfers between devices, per_device(): high = lax.ppermute(own, PLANE, second_axis_xor(2))  4.04 us
  transfers between devices with their start and end apart: 7, of which 4 were waited for; matrix products, arithmetic and copies ran while one was open for 0% of the time, Pallas kernels for 6%

profile of v3, /device:TPU:8, one launch (start us, length us, event | category | flops | bytes accessed | tf_op | source)
XLA Modules:
  0.0 67.7 jit_solution(1566813997153997161)
XLA Ops:
  0.0 0.8 %copy_bitcast_fusion = (bf16[1,16,8,128]{3,1,0,2:T(8,128)(2,1)S(1)}, bf16[1,16,8,128]{3,1,0,2:T(8,128)(2,1)S(1)}) fusion(bf16[1,1,16,8,128]{4,3,2,1,0:T(8,128)(2,1)} %param.6, bf16[1,1,16,8,128]{4,3,2,1,0:T(8,128)(2,1)} %param.5), kind=kLoop, calls=%fused_computation.5 | loop fusion | bytes 131072 | tf_op jit(solution)/shard_map/stack;squeeze | solution.py:216
  0.8 1.9 %collective-permute-start.2 = (bf16[4,2,16,128]{3,2,1,0:T(8,128)(2,1)S(1)}, bf16[4,2,16,128]{3,2,1,0:T(8,128)(2,1)S(1)}, u32[]{:S(2)}, u32[]{:S(2)}) collective-permute-start(bf16[4,2,16,128]{3,2,1,0:T(8,128)(2,1)S(1)} %broadcast_select_fusion), channel_id=1, source_target_pairs={{0,64},{64,0},{1,65},{65,1},{2,66},{66,2},{3,67},{67,3},{4,68},{68... | collective-permute-start | bytes 98312 | tf_op jit(solution)/shard_map/ppermute | solution.py:209
  2.8 1.2 %collective-permute-done.2 = bf16[4,2,16,128]{3,2,1,0:T(8,128)(2,1)S(1)} collective-permute-done((bf16[4,2,16,128]{3,2,1,0:T(8,128)(2,1)S(1)}, bf16[4,2,16,128]{3,2,1,0:T(8,128)(2,1)S(1)}, u32[]{:S(2)}, u32[]{:S(2)}) %collective-permute-start.2) | collective-permute-done | bytes 32800 | tf_op jit(solution)/shard_map/ppermute | solution.py:209
  4.0 0.8 %broadcast_in_dim.2 = bf16[4,4,2,2,16,128]{5,4,3,2,1,0:T(8,128)(2,1)} broadcast(bf16[4,2,2,16,128]{4,3,2,1,0:T(8,128)(2,1)S(1)} %copy.10), dimensions={0,2,3,4,5} | broadcast | bytes 327680 | tf_op jit(solution)/shard_map/broadcast_in_dim | solution.py:224
  4.7 0.0 copy-start.1
  4.7 13.0 %all-to-all-start = ((bf16[16,2,2,16,128]{4,3,2,1,0:T(8,128)(2,1)}), bf16[16,2,2,16,128]{4,3,2,1,0:T(8,128)(2,1)S(1)}, u32[]{:S(2)}, u32[]{:S(2)}) async-start(bf16[16,2,2,16,128]{4,3,2,1,0:T(8,128)(2,1)} %bitcast.34), calls=%async_computation | async-start | bytes 524288 | tf_op jit(solution)/shard_map/all_to_all | solution.py:225
  17.7 0.0 copy-done.1
  17.7 2.4 %collective-permute-start = (bf16[3,128,128]{2,1,0:T(8,128)(2,1)S(1)}, bf16[3,128,128]{2,1,0:T(8,128)(2,1)S(1)}, u32[]{:S(2)}, u32[]{:S(2)}) collective-permute-start(bf16[3,128,128]{2,1,0:T(8,128)(2,1)S(1)} %bitcast.61), channel_id=1, source_target_pairs={{0,1},{1,0},{2,3},{3,2},{4,5},{5,4},{6,7},{7,6},{8,9},{9,8},{10,11... | collective-permute-start | bytes 294920 | tf_op jit(solution)/shard_map/ppermute | solution.py:209
  20.1 9.9 %all-to-all-done = bf16[16,2,2,16,128]{4,3,2,1,0:T(8,128)(2,1)S(1)} async-done(((bf16[16,2,2,16,128]{4,3,2,1,0:T(8,128)(2,1)}), bf16[16,2,2,16,128]{4,3,2,1,0:T(8,128)(2,1)S(1)}, u32[]{:S(2)}, u32[]{:S(2)}) %all-to-all-start) | async-done | bytes 262176 | tf_op jit(solution)/shard_map/all_to_all | solution.py:225
  30.1 5.3 %collective-permute-start.3 = (bf16[16,2,2,16,128]{4,3,2,1,0:T(8,128)(2,1)S(1)}, bf16[16,2,2,16,128]{4,3,2,1,0:T(8,128)(2,1)S(1)}, u32[]{:S(2)}, u32[]{:S(2)}) collective-permute-start(bf16[16,2,2,16,128]{4,3,2,1,0:T(8,128)(2,1)S(1)} %all-to-all-done), channel_id=1, source_target_pairs={{0,34},{4,38},{8,42},{12,46},{16,50},{20,54},{24,58},{28,62},{1,35... | collective-permute-start | bytes 786440 | tf_op jit(solution)/shard_map/ppermute | solution.py:231
  35.3 4.0 %collective-permute-start.5 = (bf16[16,2,2,16,128]{4,3,2,1,0:T(8,128)(2,1)S(1)}, bf16[16,2,2,16,128]{4,3,2,1,0:T(8,128)(2,1)S(1)}, u32[]{:S(2)}, u32[]{:S(2)}) collective-permute-start(bf16[16,2,2,16,128]{4,3,2,1,0:T(8,128)(2,1)S(1)} %all-to-all-done), channel_id=1, source_target_pairs={{0,2},{4,6},{8,10},{12,14},{16,18},{20,22},{24,26},{28,30},{1,3},{... | collective-permute-start | bytes 786440 | tf_op jit(solution)/shard_map/ppermute | solution.py:232
  39.4 0.0 collective-permute-done
  39.4 2.9 %collective-permute-start.1 = (bf16[2,3,128,128]{3,2,1,0:T(8,128)(2,1)S(1)}, bf16[2,3,128,128]{3,2,1,0:T(8,128)(2,1)S(1)}, u32[]{:S(2)}, u32[]{:S(2)}) collective-permute-start(bf16[2,3,128,128]{3,2,1,0:T(8,128)(2,1)S(1)} %pad_maximum_fusion.qa_ref), channel_id=1, source_target_pairs={{0,4},{4,0},{1,5},{5,1},{2,6},{6,2},{3,7},{7,3},{8,12},{12,8},{9,1... | collective-permute-start | bytes 589832 | tf_op jit(solution)/shard_map/ppermute | solution.py:209
  42.3 1.1 %collective-permute-done.3 = bf16[16,2,2,16,128]{4,3,2,1,0:T(8,128)(2,1)S(1)} collective-permute-done((bf16[16,2,2,16,128]{4,3,2,1,0:T(8,128)(2,1)S(1)}, bf16[16,2,2,16,128]{4,3,2,1,0:T(8,128)(2,1)S(1)}, u32[]{:S(2)}, u32[]{:S(2)}) %collective-permute-start.3) | collective-permute-done | bytes 262176 | tf_op jit(solution)/shard_map/ppermute | solution.py:231
  43.3 2.7 %collective-permute-start.4 = (bf16[16,2,2,16,128]{4,3,2,1,0:T(8,128)(2,1)S(1)}, bf16[16,2,2,16,128]{4,3,2,1,0:T(8,128)(2,1)S(1)}, u32[]{:S(2)}, u32[]{:S(2)}) collective-permute-start(bf16[16,2,2,16,128]{4,3,2,1,0:T(8,128)(2,1)S(1)} %collective-permute-done.3), channel_id=1, source_target_pairs={{0,2},{4,6},{8,10},{12,14},{16,18},{20,22},{24,26},{28,30},{1,3},{... | collective-permute-start | bytes 786440 | tf_op jit(solution)/shard_map/ppermute | solution.py:233
  46.0 0.0 copy-start
  46.4 0.1 stack.112.place_ref
  46.5 3.8 %collective-permute-done.1.qb_ref = bf16[2,3,128,128]{3,2,1,0:T(8,128)(2,1)S(1)} collective-permute-done((bf16[2,3,128,128]{3,2,1,0:T(8,128)(2,1)S(1)}, bf16[2,3,128,128]{3,2,1,0:T(8,128)(2,1)S(1)}, u32[]{:S(2)}, u32[]{:S(2)}) %collective-permute-start.1) | collective-permute-done | bytes 196640 | tf_op jit(solution)/shard_map/ppermute | solution.py:209
  50.3 0.0 collective-permute-done.5
  50.3 0.0 copy-done
  50.3 4.0 %attend.1 = (f32[4,384,128]{2,1,0:T(8,128)S(1)}, f32[4,384,128]{2,1,0:T(8,128)S(1)}, f32[4,384,128]{2,1,0:T(8,128)S(1)}) custom-call(s32[24]{0:T(128)S(1)} %stack.112.place_ref, bf16[2,3,128,128]{3,2,1,0:T(8,128)(2,1)S(1)} %pad_maximum_fusion.qa_ref, bf16[2,3,128,128]{3,2,1,0:T(8,128)(2,1)S(1)} %collective-permute-done.1.qb_ref, s32[3,128,128]{2,1,0:T(8,128)S(1)} %copy-done, ...), custom_call_target="tpu_custom_call" | custom-call | flops 2415919104 | bytes 1048576 | tf_op jit(solution)/shard_map/attend/pallas_call | solution.py:157
  54.3 0.0 collective-permute-done.4
  54.4 3.2 %attend_last.1 = bf16[4,400,128]{2,1,0:T(8,128)(2,1)S(1)} custom-call(s32[24]{0:T(128)S(1)} %stack.112.place_ref, bf16[2,3,128,128]{3,2,1,0:T(8,128)(2,1)S(1)} %pad_maximum_fusion.qa_ref, bf16[2,3,128,128]{3,2,1,0:T(8,128)(2,1)S(1)} %collective-permute-done.1.qb_ref, s32[3,128,128]{2,1,0:T(8,128)S(1)} %copy-done, ...), custom_call_target="tpu_custom_call" | custom-call | flops 805306368 | bytes 1048576 | tf_op jit(solution)/shard_map/attend_last/pallas_call | solution.py:157
  57.6 9.1 %all_to_all.10.p_ref = bf16[4,400,128]{2,1,0:T(8,128)(2,1)S(1)} all-to-all(bf16[4,400,128]{2,1,0:T(8,128)(2,1)S(1)} %attend_last.1), channel_id=1, replica_groups=mesh['x'=4,'c'=2,'yh'=2,'zs'=4,'z0'=2,'ys'=2,'y0'=2] {'z0','y0'}, dimensions={0} | all-to-all | bytes 819200 | tf_op jit(solution)/shard_map/all_to_all | solution.py:250
  66.7 1.1 %combine.1 = bf16[3,128,128]{2,1,0:T(8,128)(2,1)} custom-call(bf16[4,400,128]{2,1,0:T(8,128)(2,1)S(1)} %all_to_all.10.p_ref), custom_call_target="tpu_custom_call" | custom-call | tf_op jit(solution)/shard_map/combine/pallas_call | solution.py:198
  (7 shorter events, 0.1 us)
Async XLA Ops:
  0.8 3.1 %collective-permute-start.2 = (bf16[4,2,16,128]{3,2,1,0:T(8,128)(2,1)S(1)}, bf16[4,2,16,128]{3,2,1,0:T(8,128)(2,1)S(1)}, u32[]{:S(2)}, u32[]{:S(2)}) collective-permute-start(bf16[4,2,16,128]{3,2,1,0:T(8,128)(2,1)S(1)} %broadcast_select_fusion), channel_id=1, source_target_pairs={{0,64},{64,0},{1,65},{65,1},{2,66},{66,2},{3,67},{67,3},{4,68},{68... | collective-permute-start | bytes 98312 | tf_op jit(solution)/shard_map/ppermute | solution.py:209
  4.7 13.0 %copy-start.1 = (bf16[128,3,128]{2,0,1:T(8,128)(2,1)S(1)}, bf16[128,3,128]{2,0,1:T(8,128)(2,1)}, u32[]{:S(2)}) copy-start(bf16[128,3,128]{2,0,1:T(8,128)(2,1)} %param.4) | copy-start | bytes 294916
  4.7 25.3 %all-to-all-start = ((bf16[16,2,2,16,128]{4,3,2,1,0:T(8,128)(2,1)}), bf16[16,2,2,16,128]{4,3,2,1,0:T(8,128)(2,1)S(1)}, u32[]{:S(2)}, u32[]{:S(2)}) async-start(bf16[16,2,2,16,128]{4,3,2,1,0:T(8,128)(2,1)} %bitcast.34), calls=%async_computation | async-start | bytes 524288 | tf_op jit(solution)/shard_map/all_to_all | solution.py:225
  17.7 21.6 %collective-permute-start = (bf16[3,128,128]{2,1,0:T(8,128)(2,1)S(1)}, bf16[3,128,128]{2,1,0:T(8,128)(2,1)S(1)}, u32[]{:S(2)}, u32[]{:S(2)}) collective-permute-start(bf16[3,128,128]{2,1,0:T(8,128)(2,1)S(1)} %bitcast.61), channel_id=1, source_target_pairs={{0,1},{1,0},{2,3},{3,2},{4,5},{5,4},{6,7},{7,6},{8,9},{9,8},{10,11... | collective-permute-start | bytes 294920 | tf_op jit(solution)/shard_map/ppermute | solution.py:209
  30.1 13.3 %collective-permute-start.3 = (bf16[16,2,2,16,128]{4,3,2,1,0:T(8,128)(2,1)S(1)}, bf16[16,2,2,16,128]{4,3,2,1,0:T(8,128)(2,1)S(1)}, u32[]{:S(2)}, u32[]{:S(2)}) collective-permute-start(bf16[16,2,2,16,128]{4,3,2,1,0:T(8,128)(2,1)S(1)} %all-to-all-done), channel_id=1, source_target_pairs={{0,34},{4,38},{8,42},{12,46},{16,50},{20,54},{24,58},{28,62},{1,35... | collective-permute-start | bytes 786440 | tf_op jit(solution)/shard_map/ppermute | solution.py:231
  35.3 15.0 %collective-permute-start.5 = (bf16[16,2,2,16,128]{4,3,2,1,0:T(8,128)(2,1)S(1)}, bf16[16,2,2,16,128]{4,3,2,1,0:T(8,128)(2,1)S(1)}, u32[]{:S(2)}, u32[]{:S(2)}) collective-permute-start(bf16[16,2,2,16,128]{4,3,2,1,0:T(8,128)(2,1)S(1)} %all-to-all-done), channel_id=1, source_target_pairs={{0,2},{4,6},{8,10},{12,14},{16,18},{20,22},{24,26},{28,30},{1,3},{... | collective-permute-start | bytes 786440 | tf_op jit(solution)/shard_map/ppermute | solution.py:232
  39.4 10.9 %collective-permute-start.1 = (bf16[2,3,128,128]{3,2,1,0:T(8,128)(2,1)S(1)}, bf16[2,3,128,128]{3,2,1,0:T(8,128)(2,1)S(1)}, u32[]{:S(2)}, u32[]{:S(2)}) collective-permute-start(bf16[2,3,128,128]{3,2,1,0:T(8,128)(2,1)S(1)} %pad_maximum_fusion.qa_ref), channel_id=1, source_target_pairs={{0,4},{4,0},{1,5},{5,1},{2,6},{6,2},{3,7},{7,3},{8,12},{12,8},{9,1... | collective-permute-start | bytes 589832 | tf_op jit(solution)/shard_map/ppermute | solution.py:209
  43.3 11.0 %collective-permute-start.4 = (bf16[16,2,2,16,128]{4,3,2,1,0:T(8,128)(2,1)S(1)}, bf16[16,2,2,16,128]{4,3,2,1,0:T(8,128)(2,1)S(1)}, u32[]{:S(2)}, u32[]{:S(2)}) collective-permute-start(bf16[16,2,2,16,128]{4,3,2,1,0:T(8,128)(2,1)S(1)} %collective-permute-done.3), channel_id=1, source_target_pairs={{0,2},{4,6},{8,10},{12,14},{16,18},{20,22},{24,26},{28,30},{1,3},{... | collective-permute-start | bytes 786440 | tf_op jit(solution)/shard_map/ppermute | solution.py:233
  46.0 4.2 %copy-start = (s32[3,128,128]{2,1,0:T(8,128)S(1)}, s32[3,128,128]{2,1,0:T(8,128)}, u32[]{:S(2)}) copy-start(s32[3,128,128]{2,1,0:T(8,128)} %mask_ref.3) | copy-start | bytes 589828

commit v4 on v3

--- a/solution.py
+++ b/solution.py
@@ -114,15 +114,21 @@
     lane, _ = load_operands(base, place_ref, qa_ref, qb_ref, mask_ref, [kv_ref], qx_ref, kx_ref, vx_ref)
     for j in range(4):
         s_ref[j] = jnp.dot(qx_ref[j], kx_ref[...], preferred_element_type=jnp.float32)
+    for j in range(4):
         slot = j ^ place_ref[5]
-        stats = []
+        stats, tops, weights = [], [], []
         for g in range(GROUP):
             rows = pl.ds(g * ROWS, ROWS)
             scores = s_ref[j, rows, :]
             before = top_in[j, rows, :]
-            highest = jnp.maximum(jnp.max(scores, axis=1, keepdims=True), before[:, :1])
-            weights = jnp.exp2((scores - highest) * SCALE2).astype(jnp.bfloat16)
-            both = jnp.dot(weights, vx_ref[...], preferred_element_type=jnp.float32)
+            highest = jnp.maximum(jnp.max(scores, axis=1, keepdims=True), before)
+            shift = jnp.concatenate([highest] * (scores.shape[1] // HD), axis=1)
+            weights.append(jnp.exp2((scores - shift) * SCALE2).astype(jnp.bfloat16))
+            tops.append(highest)
+        total = jnp.dot(jnp.concatenate(weights, axis=0), vx_ref[...], preferred_element_type=jnp.float32)
+        for g in range(GROUP):
+            rows = pl.ds(g * ROWS, ROWS)
+            both, before, highest = total[g * ROWS : (g + 1) * ROWS], top_in[j, rows, :], tops[g]
             keep = jnp.exp2((before - highest) * SCALE2)
             acc = both[:, :HD] + keep * acc_in[j, rows, :]
             denominator = both[:, HD:] + keep * den_in[j, rows, :]

time: 68.2 us -> 67.2 us (0.985)
  Pallas kernels: 8.32 us -> 7.31 us
    pallas_call x2, Pallas kernels: 7.25 us -> 6.24 us  [attend(): pl.pallas_call(kernel, out_shape=outs, in_specs=[pl.BlockSpec(memory_spac...]
where the time goes in v4:
time: 67.2 us; the launch traced here: 66.7 us
  starting transfers between devices  32.1 us (48%)
  waiting for transfers between devices  16 us (24%)
  blocking collectives  9.1 us (14%)
  Pallas kernels  7.31 us (11%)
  local copies, waits for them, and re-layouts  1.67 us (2%)
    all_to_all x1, starting transfers between devices, per_device(): lax.all_to_all(kv, AXES, 0, 0, axis_index_groups=first_axis_groups(), til...  13 us
    all_to_all x1, waiting for transfers between devices, per_device(): lax.all_to_all(kv, AXES, 0, 0, axis_index_groups=first_axis_groups(), til...  9.95 us
    all_to_all x1, blocking collectives, per_device(): parts = lax.all_to_all(parts, BLOCK, 0, 0, tiled=True)  9.1 us
    ppermute x3, starting transfers between devices, swap(): return lax.ppermute(value, axis, [(0, 1), (1, 0)])  7.13 us
    pallas_call x2, Pallas kernels, attend(): pl.pallas_call(kernel, out_shape=outs, in_specs=[pl.BlockSpec(memory_spac...  6.24 us
    ppermute x1, starting transfers between devices, per_device(): low = lax.ppermute(own, PLANE, second_axis_xor(6))  5.25 us
    ppermute x3, waiting for transfers between devices, swap(): return lax.ppermute(value, axis, [(0, 1), (1, 0)])  4.99 us
    ppermute x1, starting transfers between devices, per_device(): high = lax.ppermute(own, PLANE, second_axis_xor(2))  4.04 us
  transfers between devices with their start and end apart: 7, of which 4 were waited for; matrix products, arithmetic and copies ran while one was open for 0% of the time, Pallas kernels for 6%

profile of v4, /device:TPU:8, one launch (start us, length us, event | category | flops | bytes accessed | tf_op | source)
XLA Modules:
  0.0 66.7 jit_solution(5553842677562145929)
XLA Ops:
  0.0 0.8 %copy_bitcast_fusion = (bf16[1,16,8,128]{3,1,0,2:T(8,128)(2,1)S(1)}, bf16[1,16,8,128]{3,1,0,2:T(8,128)(2,1)S(1)}) fusion(bf16[1,1,16,8,128]{4,3,2,1,0:T(8,128)(2,1)} %param.6, bf16[1,1,16,8,128]{4,3,2,1,0:T(8,128)(2,1)} %param.5), kind=kLoop, calls=%fused_computation.5 | loop fusion | bytes 131072 | tf_op jit(solution)/shard_map/stack;squeeze | solution.py:222
  0.8 1.9 %collective-permute-start.2 = (bf16[4,2,16,128]{3,2,1,0:T(8,128)(2,1)S(1)}, bf16[4,2,16,128]{3,2,1,0:T(8,128)(2,1)S(1)}, u32[]{:S(2)}, u32[]{:S(2)}) collective-permute-start(bf16[4,2,16,128]{3,2,1,0:T(8,128)(2,1)S(1)} %broadcast_select_fusion), channel_id=1, source_target_pairs={{0,64},{64,0},{1,65},{65,1},{2,66},{66,2},{3,67},{67,3},{4,68},{68... | collective-permute-start | bytes 98312 | tf_op jit(solution)/shard_map/ppermute | solution.py:215
  2.8 1.2 %collective-permute-done.2 = bf16[4,2,16,128]{3,2,1,0:T(8,128)(2,1)S(1)} collective-permute-done((bf16[4,2,16,128]{3,2,1,0:T(8,128)(2,1)S(1)}, bf16[4,2,16,128]{3,2,1,0:T(8,128)(2,1)S(1)}, u32[]{:S(2)}, u32[]{:S(2)}) %collective-permute-start.2) | collective-permute-done | bytes 32800 | tf_op jit(solution)/shard_map/ppermute | solution.py:215
  4.0 0.8 %broadcast_in_dim.2 = bf16[4,4,2,2,16,128]{5,4,3,2,1,0:T(8,128)(2,1)} broadcast(bf16[4,2,2,16,128]{4,3,2,1,0:T(8,128)(2,1)S(1)} %copy.10), dimensions={0,2,3,4,5} | broadcast | bytes 327680 | tf_op jit(solution)/shard_map/broadcast_in_dim | solution.py:230
  4.7 0.0 copy-start.1
  4.7 13.0 %all-to-all-start = ((bf16[16,2,2,16,128]{4,3,2,1,0:T(8,128)(2,1)}), bf16[16,2,2,16,128]{4,3,2,1,0:T(8,128)(2,1)S(1)}, u32[]{:S(2)}, u32[]{:S(2)}) async-start(bf16[16,2,2,16,128]{4,3,2,1,0:T(8,128)(2,1)} %bitcast.34), calls=%async_computation | async-start | bytes 524288 | tf_op jit(solution)/shard_map/all_to_all | solution.py:231
  17.7 0.0 copy-done.1
  17.7 2.4 %collective-permute-start = (bf16[3,128,128]{2,1,0:T(8,128)(2,1)S(1)}, bf16[3,128,128]{2,1,0:T(8,128)(2,1)S(1)}, u32[]{:S(2)}, u32[]{:S(2)}) collective-permute-start(bf16[3,128,128]{2,1,0:T(8,128)(2,1)S(1)} %bitcast.61), channel_id=1, source_target_pairs={{0,1},{1,0},{2,3},{3,2},{4,5},{5,4},{6,7},{7,6},{8,9},{9,8},{10,11... | collective-permute-start | bytes 294920 | tf_op jit(solution)/shard_map/ppermute | solution.py:215
  20.1 9.9 %all-to-all-done = bf16[16,2,2,16,128]{4,3,2,1,0:T(8,128)(2,1)S(1)} async-done(((bf16[16,2,2,16,128]{4,3,2,1,0:T(8,128)(2,1)}), bf16[16,2,2,16,128]{4,3,2,1,0:T(8,128)(2,1)S(1)}, u32[]{:S(2)}, u32[]{:S(2)}) %all-to-all-start) | async-done | bytes 262176 | tf_op jit(solution)/shard_map/all_to_all | solution.py:231
  30.1 5.3 %collective-permute-start.3 = (bf16[16,2,2,16,128]{4,3,2,1,0:T(8,128)(2,1)S(1)}, bf16[16,2,2,16,128]{4,3,2,1,0:T(8,128)(2,1)S(1)}, u32[]{:S(2)}, u32[]{:S(2)}) collective-permute-start(bf16[16,2,2,16,128]{4,3,2,1,0:T(8,128)(2,1)S(1)} %all-to-all-done), channel_id=1, source_target_pairs={{0,34},{4,38},{8,42},{12,46},{16,50},{20,54},{24,58},{28,62},{1,35... | collective-permute-start | bytes 786440 | tf_op jit(solution)/shard_map/ppermute | solution.py:237
  35.3 4.0 %collective-permute-start.5 = (bf16[16,2,2,16,128]{4,3,2,1,0:T(8,128)(2,1)S(1)}, bf16[16,2,2,16,128]{4,3,2,1,0:T(8,128)(2,1)S(1)}, u32[]{:S(2)}, u32[]{:S(2)}) collective-permute-start(bf16[16,2,2,16,128]{4,3,2,1,0:T(8,128)(2,1)S(1)} %all-to-all-done), channel_id=1, source_target_pairs={{0,2},{4,6},{8,10},{12,14},{16,18},{20,22},{24,26},{28,30},{1,3},{... | collective-permute-start | bytes 786440 | tf_op jit(solution)/shard_map/ppermute | solution.py:238
  39.4 0.0 collective-permute-done
  39.4 2.9 %collective-permute-start.1 = (bf16[2,3,128,128]{3,2,1,0:T(8,128)(2,1)S(1)}, bf16[2,3,128,128]{3,2,1,0:T(8,128)(2,1)S(1)}, u32[]{:S(2)}, u32[]{:S(2)}) collective-permute-start(bf16[2,3,128,128]{3,2,1,0:T(8,128)(2,1)S(1)} %pad_maximum_fusion.qa_ref), channel_id=1, source_target_pairs={{0,4},{4,0},{1,5},{5,1},{2,6},{6,2},{3,7},{7,3},{8,12},{12,8},{9,1... | collective-permute-start | bytes 589832 | tf_op jit(solution)/shard_map/ppermute | solution.py:215
  42.3 1.1 %collective-permute-done.3 = bf16[16,2,2,16,128]{4,3,2,1,0:T(8,128)(2,1)S(1)} collective-permute-done((bf16[16,2,2,16,128]{4,3,2,1,0:T(8,128)(2,1)S(1)}, bf16[16,2,2,16,128]{4,3,2,1,0:T(8,128)(2,1)S(1)}, u32[]{:S(2)}, u32[]{:S(2)}) %collective-permute-start.3) | collective-permute-done | bytes 262176 | tf_op jit(solution)/shard_map/ppermute | solution.py:237
  43.3 2.7 %collective-permute-start.4 = (bf16[16,2,2,16,128]{4,3,2,1,0:T(8,128)(2,1)S(1)}, bf16[16,2,2,16,128]{4,3,2,1,0:T(8,128)(2,1)S(1)}, u32[]{:S(2)}, u32[]{:S(2)}) collective-permute-start(bf16[16,2,2,16,128]{4,3,2,1,0:T(8,128)(2,1)S(1)} %collective-permute-done.3), channel_id=1, source_target_pairs={{0,2},{4,6},{8,10},{12,14},{16,18},{20,22},{24,26},{28,30},{1,3},{... | collective-permute-start | bytes 786440 | tf_op jit(solution)/shard_map/ppermute | solution.py:239
  46.0 0.0 copy-start
  46.4 0.1 stack.112.place_ref
  46.5 3.8 %collective-permute-done.1.qb_ref = bf16[2,3,128,128]{3,2,1,0:T(8,128)(2,1)S(1)} collective-permute-done((bf16[2,3,128,128]{3,2,1,0:T(8,128)(2,1)S(1)}, bf16[2,3,128,128]{3,2,1,0:T(8,128)(2,1)S(1)}, u32[]{:S(2)}, u32[]{:S(2)}) %collective-permute-start.1) | collective-permute-done | bytes 196640 | tf_op jit(solution)/shard_map/ppermute | solution.py:215
  50.3 0.0 collective-permute-done.5
  50.3 0.0 copy-done
  50.3 4.0 %attend.1 = (f32[4,384,128]{2,1,0:T(8,128)S(1)}, f32[4,384,128]{2,1,0:T(8,128)S(1)}, f32[4,384,128]{2,1,0:T(8,128)S(1)}) custom-call(s32[24]{0:T(128)S(1)} %stack.112.place_ref, bf16[2,3,128,128]{3,2,1,0:T(8,128)(2,1)S(1)} %pad_maximum_fusion.qa_ref, bf16[2,3,128,128]{3,2,1,0:T(8,128)(2,1)S(1)} %collective-permute-done.1.qb_ref, s32[3,128,128]{2,1,0:T(8,128)S(1)} %copy-done, ...), custom_call_target="tpu_custom_call" | custom-call | flops 2415919104 | bytes 1048576 | tf_op jit(solution)/shard_map/attend/pallas_call | solution.py:163
  54.3 0.0 collective-permute-done.4
  54.4 2.2 %attend_last.1 = bf16[4,400,128]{2,1,0:T(8,128)(2,1)S(1)} custom-call(s32[24]{0:T(128)S(1)} %stack.112.place_ref, bf16[2,3,128,128]{3,2,1,0:T(8,128)(2,1)S(1)} %pad_maximum_fusion.qa_ref, bf16[2,3,128,128]{3,2,1,0:T(8,128)(2,1)S(1)} %collective-permute-done.1.qb_ref, s32[3,128,128]{2,1,0:T(8,128)S(1)} %copy-done, ...), custom_call_target="tpu_custom_call" | custom-call | flops 805306368 | bytes 1048576 | tf_op jit(solution)/shard_map/attend_last/pallas_call | solution.py:163
  56.6 9.1 %all_to_all.10.p_ref = bf16[4,400,128]{2,1,0:T(8,128)(2,1)S(1)} all-to-all(bf16[4,400,128]{2,1,0:T(8,128)(2,1)S(1)} %attend_last.1), channel_id=1, replica_groups=mesh['x'=4,'c'=2,'yh'=2,'zs'=4,'z0'=2,'ys'=2,'y0'=2] {'z0','y0'}, dimensions={0} | all-to-all | bytes 819200 | tf_op jit(solution)/shard_map/all_to_all | solution.py:256
  65.7 1.1 %combine.1 = bf16[3,128,128]{2,1,0:T(8,128)(2,1)} custom-call(bf16[4,400,128]{2,1,0:T(8,128)(2,1)S(1)} %all_to_all.10.p_ref), custom_call_target="tpu_custom_call" | custom-call | tf_op jit(solution)/shard_map/combine/pallas_call | solution.py:204
  (7 shorter events, 0.1 us)
Async XLA Ops:
  0.8 3.1 %collective-permute-start.2 = (bf16[4,2,16,128]{3,2,1,0:T(8,128)(2,1)S(1)}, bf16[4,2,16,128]{3,2,1,0:T(8,128)(2,1)S(1)}, u32[]{:S(2)}, u32[]{:S(2)}) collective-permute-start(bf16[4,2,16,128]{3,2,1,0:T(8,128)(2,1)S(1)} %broadcast_select_fusion), channel_id=1, source_target_pairs={{0,64},{64,0},{1,65},{65,1},{2,66},{66,2},{3,67},{67,3},{4,68},{68... | collective-permute-start | bytes 98312 | tf_op jit(solution)/shard_map/ppermute | solution.py:215
  4.7 13.0 %copy-start.1 = (bf16[128,3,128]{2,0,1:T(8,128)(2,1)S(1)}, bf16[128,3,128]{2,0,1:T(8,128)(2,1)}, u32[]{:S(2)}) copy-start(bf16[128,3,128]{2,0,1:T(8,128)(2,1)} %param.4) | copy-start | bytes 294916
  4.7 25.3 %all-to-all-start = ((bf16[16,2,2,16,128]{4,3,2,1,0:T(8,128)(2,1)}), bf16[16,2,2,16,128]{4,3,2,1,0:T(8,128)(2,1)S(1)}, u32[]{:S(2)}, u32[]{:S(2)}) async-start(bf16[16,2,2,16,128]{4,3,2,1,0:T(8,128)(2,1)} %bitcast.34), calls=%async_computation | async-start | bytes 524288 | tf_op jit(solution)/shard_map/all_to_all | solution.py:231
  17.7 21.6 %collective-permute-start = (bf16[3,128,128]{2,1,0:T(8,128)(2,1)S(1)}, bf16[3,128,128]{2,1,0:T(8,128)(2,1)S(1)}, u32[]{:S(2)}, u32[]{:S(2)}) collective-permute-start(bf16[3,128,128]{2,1,0:T(8,128)(2,1)S(1)} %bitcast.61), channel_id=1, source_target_pairs={{0,1},{1,0},{2,3},{3,2},{4,5},{5,4},{6,7},{7,6},{8,9},{9,8},{10,11... | collective-permute-start | bytes 294920 | tf_op jit(solution)/shard_map/ppermute | solution.py:215
  30.1 13.3 %collective-permute-start.3 = (bf16[16,2,2,16,128]{4,3,2,1,0:T(8,128)(2,1)S(1)}, bf16[16,2,2,16,128]{4,3,2,1,0:T(8,128)(2,1)S(1)}, u32[]{:S(2)}, u32[]{:S(2)}) collective-permute-start(bf16[16,2,2,16,128]{4,3,2,1,0:T(8,128)(2,1)S(1)} %all-to-all-done), channel_id=1, source_target_pairs={{0,34},{4,38},{8,42},{12,46},{16,50},{20,54},{24,58},{28,62},{1,35... | collective-permute-start | bytes 786440 | tf_op jit(solution)/shard_map/ppermute | solution.py:237
  35.3 15.0 %collective-permute-start.5 = (bf16[16,2,2,16,128]{4,3,2,1,0:T(8,128)(2,1)S(1)}, bf16[16,2,2,16,128]{4,3,2,1,0:T(8,128)(2,1)S(1)}, u32[]{:S(2)}, u32[]{:S(2)}) collective-permute-start(bf16[16,2,2,16,128]{4,3,2,1,0:T(8,128)(2,1)S(1)} %all-to-all-done), channel_id=1, source_target_pairs={{0,2},{4,6},{8,10},{12,14},{16,18},{20,22},{24,26},{28,30},{1,3},{... | collective-permute-start | bytes 786440 | tf_op jit(solution)/shard_map/ppermute | solution.py:238
  39.4 10.9 %collective-permute-start.1 = (bf16[2,3,128,128]{3,2,1,0:T(8,128)(2,1)S(1)}, bf16[2,3,128,128]{3,2,1,0:T(8,128)(2,1)S(1)}, u32[]{:S(2)}, u32[]{:S(2)}) collective-permute-start(bf16[2,3,128,128]{3,2,1,0:T(8,128)(2,1)S(1)} %pad_maximum_fusion.qa_ref), channel_id=1, source_target_pairs={{0,4},{4,0},{1,5},{5,1},{2,6},{6,2},{3,7},{7,3},{8,12},{12,8},{9,1... | collective-permute-start | bytes 589832 | tf_op jit(solution)/shard_map/ppermute | solution.py:215
  43.3 11.0 %collective-permute-start.4 = (bf16[16,2,2,16,128]{4,3,2,1,0:T(8,128)(2,1)S(1)}, bf16[16,2,2,16,128]{4,3,2,1,0:T(8,128)(2,1)S(1)}, u32[]{:S(2)}, u32[]{:S(2)}) collective-permute-start(bf16[16,2,2,16,128]{4,3,2,1,0:T(8,128)(2,1)S(1)} %collective-permute-done.3), channel_id=1, source_target_pairs={{0,2},{4,6},{8,10},{12,14},{16,18},{20,22},{24,26},{28,30},{1,3},{... | collective-permute-start | bytes 786440 | tf_op jit(solution)/shard_map/ppermute | solution.py:239
  46.0 4.2 %copy-start = (s32[3,128,128]{2,1,0:T(8,128)S(1)}, s32[3,128,128]{2,1,0:T(8,128)}, u32[]{:S(2)}) copy-start(s32[3,128,128]{2,1,0:T(8,128)} %mask_ref.3) | copy-start | bytes 589828

commit v5 on v4

--- a/solution.py
+++ b/solution.py
@@ -35,11 +35,12 @@
     return [(c, y, z) for c in range(2) for y in range(8) for z in range(8)]
 
 
-def second_axis_xor(bits):
+def second_axis_xor(bits, relay=False):
     pairs = []
     for c, y, z in plane_places():
         to = (y ^ bits, z) if c == 0 else (y, z ^ bits)
-        pairs.append((plane_index(c, y, z), plane_index(c, *to)))
+        if c == 1 or (y >= 4 if relay else to[0] >= 4 or y < 4):
+            pairs.append((plane_index(c, y, z), plane_index(c, *to)))
     return pairs
 
 
@@ -236,7 +237,7 @@
 
     low = lax.ppermute(own, PLANE, second_axis_xor(6))
     high = lax.ppermute(own, PLANE, second_axis_xor(2))
-    far = lax.ppermute(low, PLANE, second_axis_xor(2))
+    far = lax.ppermute(low, PLANE, second_axis_xor(2, relay=True))
     own, low, high, far = (a.reshape(4, FAR, 2, 2, 16, HD) for a in (own, low, high, far))
 
     q_shards = [shard_of(y ^ (j & 1), z ^ (j >> 1)) for j in range(4)]

time: 67.2 us -> 67.2 us (level)
  starting transfers between devices: 32.1 us -> 30.1 us
  waiting for transfers between devices: 16 us -> 18 us
    ppermute x3, waiting for transfers between devices: 4.99 us -> 8.06 us  [swap(): return lax.ppermute(value, axis, [(0, 1), (1, 0)])]
    ppermute x1, starting transfers between devices: 2.7 us -> 0.68 us  [per_device(): far = lax.ppermute(low, PLANE, second_axis_xor(2, relay=True))]
    ppermute x1, waiting for transfers between devices: 1.06 us -> 0.01 us  [per_device(): low = lax.ppermute(own, PLANE, second_axis_xor(6))]
  transfers between devices with their start and end apart: 7 -> 7, of which waited for: 4 -> 3; matrix products, arithmetic and copies ran while one was open for 0% -> 0% of each run, Pallas kernels for 6% -> 6%
where the time goes in v5:
time: 67.2 us; the launch traced here: 66.7 us
  starting transfers between devices  30.1 us (45%)
  waiting for transfers between devices  18 us (27%)
  blocking collectives  9.08 us (14%)
  Pallas kernels  7.32 us (11%)
  local copies, waits for them, and re-layouts  1.67 us (2%)
    all_to_all x1, starting transfers between devices, per_device(): lax.all_to_all(kv, AXES, 0, 0, axis_index_groups=first_axis_groups(), til...  13 us
    all_to_all x1, waiting for transfers between devices, per_device(): lax.all_to_all(kv, AXES, 0, 0, axis_index_groups=first_axis_groups(), til...  9.95 us
    all_to_all x1, blocking collectives, per_device(): parts = lax.all_to_all(parts, BLOCK, 0, 0, tiled=True)  9.08 us
    ppermute x3, waiting for transfers between devices, swap(): return lax.ppermute(value, axis, [(0, 1), (1, 0)])  8.06 us
    ppermute x3, starting transfers between devices, swap(): return lax.ppermute(value, axis, [(0, 1), (1, 0)])  7.13 us
    pallas_call x2, Pallas kernels, attend(): pl.pallas_call(kernel, out_shape=outs, in_specs=[pl.BlockSpec(memory_spac...  6.25 us
    ppermute x1, starting transfers between devices, per_device(): low = lax.ppermute(own, PLANE, second_axis_xor(6))  5.26 us
    ppermute x1, starting transfers between devices, per_device(): high = lax.ppermute(own, PLANE, second_axis_xor(2))  4.04 us
  transfers between devices with their start and end apart: 7, of which 3 were waited for; matrix products, arithmetic and copies ran while one was open for 0% of the time, Pallas kernels for 6%

profile of v5, /device:TPU:8, one launch (start us, length us, event | category | flops | bytes accessed | tf_op | source)
XLA Modules:
  0.0 66.7 jit_solution(6158288743877551890)
XLA Ops:
  0.0 0.8 %copy_bitcast_fusion = (bf16[1,16,8,128]{3,1,0,2:T(8,128)(2,1)S(1)}, bf16[1,16,8,128]{3,1,0,2:T(8,128)(2,1)S(1)}) fusion(bf16[1,1,16,8,128]{4,3,2,1,0:T(8,128)(2,1)} %param.6, bf16[1,1,16,8,128]{4,3,2,1,0:T(8,128)(2,1)} %param.5), kind=kLoop, calls=%fused_computation.5 | loop fusion | bytes 131072 | tf_op jit(solution)/shard_map/stack;squeeze | solution.py:223
  0.8 1.9 %collective-permute-start.2 = (bf16[4,2,16,128]{3,2,1,0:T(8,128)(2,1)S(1)}, bf16[4,2,16,128]{3,2,1,0:T(8,128)(2,1)S(1)}, u32[]{:S(2)}, u32[]{:S(2)}) collective-permute-start(bf16[4,2,16,128]{3,2,1,0:T(8,128)(2,1)S(1)} %broadcast_select_fusion), channel_id=1, source_target_pairs={{0,64},{64,0},{1,65},{65,1},{2,66},{66,2},{3,67},{67,3},{4,68},{68... | collective-permute-start | bytes 98312 | tf_op jit(solution)/shard_map/ppermute | solution.py:216
  2.8 1.2 %collective-permute-done.2 = bf16[4,2,16,128]{3,2,1,0:T(8,128)(2,1)S(1)} collective-permute-done((bf16[4,2,16,128]{3,2,1,0:T(8,128)(2,1)S(1)}, bf16[4,2,16,128]{3,2,1,0:T(8,128)(2,1)S(1)}, u32[]{:S(2)}, u32[]{:S(2)}) %collective-permute-start.2) | collective-permute-done | bytes 32800 | tf_op jit(solution)/shard_map/ppermute | solution.py:216
  4.0 0.8 %broadcast_in_dim.2 = bf16[4,4,2,2,16,128]{5,4,3,2,1,0:T(8,128)(2,1)} broadcast(bf16[4,2,2,16,128]{4,3,2,1,0:T(8,128)(2,1)S(1)} %copy.10), dimensions={0,2,3,4,5} | broadcast | bytes 327680 | tf_op jit(solution)/shard_map/broadcast_in_dim | solution.py:231
  4.7 0.0 copy-start.1
  4.7 13.0 %all-to-all-start = ((bf16[16,2,2,16,128]{4,3,2,1,0:T(8,128)(2,1)}), bf16[16,2,2,16,128]{4,3,2,1,0:T(8,128)(2,1)S(1)}, u32[]{:S(2)}, u32[]{:S(2)}) async-start(bf16[16,2,2,16,128]{4,3,2,1,0:T(8,128)(2,1)} %bitcast.34), calls=%async_computation | async-start | bytes 524288 | tf_op jit(solution)/shard_map/all_to_all | solution.py:232
  17.7 0.0 copy-done.1
  17.7 2.4 %collective-permute-start = (bf16[3,128,128]{2,1,0:T(8,128)(2,1)S(1)}, bf16[3,128,128]{2,1,0:T(8,128)(2,1)S(1)}, u32[]{:S(2)}, u32[]{:S(2)}) collective-permute-start(bf16[3,128,128]{2,1,0:T(8,128)(2,1)S(1)} %bitcast.61), channel_id=1, source_target_pairs={{0,1},{1,0},{2,3},{3,2},{4,5},{5,4},{6,7},{7,6},{8,9},{9,8},{10,11... | collective-permute-start | bytes 294920 | tf_op jit(solution)/shard_map/ppermute | solution.py:216
  20.1 9.9 %all-to-all-done = bf16[16,2,2,16,128]{4,3,2,1,0:T(8,128)(2,1)S(1)} async-done(((bf16[16,2,2,16,128]{4,3,2,1,0:T(8,128)(2,1)}), bf16[16,2,2,16,128]{4,3,2,1,0:T(8,128)(2,1)S(1)}, u32[]{:S(2)}, u32[]{:S(2)}) %all-to-all-start) | async-done | bytes 262176 | tf_op jit(solution)/shard_map/all_to_all | solution.py:232
  30.1 5.3 %collective-permute-start.3 = (bf16[16,2,2,16,128]{4,3,2,1,0:T(8,128)(2,1)S(1)}, bf16[16,2,2,16,128]{4,3,2,1,0:T(8,128)(2,1)S(1)}, u32[]{:S(2)}, u32[]{:S(2)}) collective-permute-start(bf16[16,2,2,16,128]{4,3,2,1,0:T(8,128)(2,1)S(1)} %all-to-all-done), channel_id=1, source_target_pairs={{0,34},{4,38},{8,42},{12,46},{16,50},{20,54},{24,58},{28,62},{1,35... | collective-permute-start | bytes 786440 | tf_op jit(solution)/shard_map/ppermute | solution.py:238
  35.3 4.0 %collective-permute-start.5 = (bf16[16,2,2,16,128]{4,3,2,1,0:T(8,128)(2,1)S(1)}, bf16[16,2,2,16,128]{4,3,2,1,0:T(8,128)(2,1)S(1)}, u32[]{:S(2)}, u32[]{:S(2)}) collective-permute-start(bf16[16,2,2,16,128]{4,3,2,1,0:T(8,128)(2,1)S(1)} %all-to-all-done), channel_id=1, source_target_pairs={{0,2},{4,6},{8,10},{12,14},{16,18},{20,22},{24,26},{28,30},{1,3},{... | collective-permute-start | bytes 786440 | tf_op jit(solution)/shard_map/ppermute | solution.py:239
  39.4 0.0 collective-permute-done
  39.4 2.9 %collective-permute-start.1 = (bf16[2,3,128,128]{3,2,1,0:T(8,128)(2,1)S(1)}, bf16[2,3,128,128]{3,2,1,0:T(8,128)(2,1)S(1)}, u32[]{:S(2)}, u32[]{:S(2)}) collective-permute-start(bf16[2,3,128,128]{3,2,1,0:T(8,128)(2,1)S(1)} %pad_maximum_fusion.qa_ref), channel_id=1, source_target_pairs={{0,4},{4,0},{1,5},{5,1},{2,6},{6,2},{3,7},{7,3},{8,12},{12,8},{9,1... | collective-permute-start | bytes 589832 | tf_op jit(solution)/shard_map/ppermute | solution.py:216
  42.3 0.0 collective-permute-done.3
  42.3 0.7 %collective-permute-start.4 = (bf16[16,2,2,16,128]{4,3,2,1,0:T(8,128)(2,1)S(1)}, bf16[16,2,2,16,128]{4,3,2,1,0:T(8,128)(2,1)S(1)}, u32[]{:S(2)}, u32[]{:S(2)}) collective-permute-start(bf16[16,2,2,16,128]{4,3,2,1,0:T(8,128)(2,1)S(1)} %collective-permute-done.3), channel_id=1, source_target_pairs={{32,34},{36,38},{40,42},{44,46},{48,50},{52,54},{56,58},{60,62},{3... | collective-permute-start | bytes 786440 | tf_op jit(solution)/shard_map/ppermute | solution.py:240
  43.0 0.0 copy-start
  43.3 0.1 stack.112.place_ref
  43.4 6.9 %collective-permute-done.1.qb_ref = bf16[2,3,128,128]{3,2,1,0:T(8,128)(2,1)S(1)} collective-permute-done((bf16[2,3,128,128]{3,2,1,0:T(8,128)(2,1)S(1)}, bf16[2,3,128,128]{3,2,1,0:T(8,128)(2,1)S(1)}, u32[]{:S(2)}, u32[]{:S(2)}) %collective-permute-start.1) | collective-permute-done | bytes 196640 | tf_op jit(solution)/shard_map/ppermute | solution.py:216
  50.3 0.0 collective-permute-done.5
  50.3 0.0 copy-done
  50.3 4.0 %attend.1 = (f32[4,384,128]{2,1,0:T(8,128)S(1)}, f32[4,384,128]{2,1,0:T(8,128)S(1)}, f32[4,384,128]{2,1,0:T(8,128)S(1)}) custom-call(s32[24]{0:T(128)S(1)} %stack.112.place_ref, bf16[2,3,128,128]{3,2,1,0:T(8,128)(2,1)S(1)} %pad_maximum_fusion.qa_ref, bf16[2,3,128,128]{3,2,1,0:T(8,128)(2,1)S(1)} %collective-permute-done.1.qb_ref, s32[3,128,128]{2,1,0:T(8,128)S(1)} %copy-done, ...), custom_call_target="tpu_custom_call" | custom-call | flops 2415919104 | bytes 1048576 | tf_op jit(solution)/shard_map/attend/pallas_call | solution.py:164
  54.4 0.0 collective-permute-done.4
  54.4 2.2 %attend_last.1 = bf16[4,400,128]{2,1,0:T(8,128)(2,1)S(1)} custom-call(s32[24]{0:T(128)S(1)} %stack.112.place_ref, bf16[2,3,128,128]{3,2,1,0:T(8,128)(2,1)S(1)} %pad_maximum_fusion.qa_ref, bf16[2,3,128,128]{3,2,1,0:T(8,128)(2,1)S(1)} %collective-permute-done.1.qb_ref, s32[3,128,128]{2,1,0:T(8,128)S(1)} %copy-done, ...), custom_call_target="tpu_custom_call" | custom-call | flops 805306368 | bytes 1048576 | tf_op jit(solution)/shard_map/attend_last/pallas_call | solution.py:164
  56.6 9.1 %all_to_all.10.p_ref = bf16[4,400,128]{2,1,0:T(8,128)(2,1)S(1)} all-to-all(bf16[4,400,128]{2,1,0:T(8,128)(2,1)S(1)} %attend_last.1), channel_id=1, replica_groups=mesh['x'=4,'c'=2,'yh'=2,'zs'=4,'z0'=2,'ys'=2,'y0'=2] {'z0','y0'}, dimensions={0} | all-to-all | bytes 819200 | tf_op jit(solution)/shard_map/all_to_all | solution.py:257
  65.7 1.1 %combine.1 = bf16[3,128,128]{2,1,0:T(8,128)(2,1)} custom-call(bf16[4,400,128]{2,1,0:T(8,128)(2,1)S(1)} %all_to_all.10.p_ref), custom_call_target="tpu_custom_call" | custom-call | tf_op jit(solution)/shard_map/combine/pallas_call | solution.py:205
  (7 shorter events, 0.1 us)
Async XLA Ops:
  0.8 3.1 %collective-permute-start.2 = (bf16[4,2,16,128]{3,2,1,0:T(8,128)(2,1)S(1)}, bf16[4,2,16,128]{3,2,1,0:T(8,128)(2,1)S(1)}, u32[]{:S(2)}, u32[]{:S(2)}) collective-permute-start(bf16[4,2,16,128]{3,2,1,0:T(8,128)(2,1)S(1)} %broadcast_select_fusion), channel_id=1, source_target_pairs={{0,64},{64,0},{1,65},{65,1},{2,66},{66,2},{3,67},{67,3},{4,68},{68... | collective-permute-start | bytes 98312 | tf_op jit(solution)/shard_map/ppermute | solution.py:216
  4.7 13.0 %copy-start.1 = (bf16[128,3,128]{2,0,1:T(8,128)(2,1)S(1)}, bf16[128,3,128]{2,0,1:T(8,128)(2,1)}, u32[]{:S(2)}) copy-start(bf16[128,3,128]{2,0,1:T(8,128)(2,1)} %param.4) | copy-start | bytes 294916
  4.7 25.3 %all-to-all-start = ((bf16[16,2,2,16,128]{4,3,2,1,0:T(8,128)(2,1)}), bf16[16,2,2,16,128]{4,3,2,1,0:T(8,128)(2,1)S(1)}, u32[]{:S(2)}, u32[]{:S(2)}) async-start(bf16[16,2,2,16,128]{4,3,2,1,0:T(8,128)(2,1)} %bitcast.34), calls=%async_computation | async-start | bytes 524288 | tf_op jit(solution)/shard_map/all_to_all | solution.py:232
  17.7 21.6 %collective-permute-start = (bf16[3,128,128]{2,1,0:T(8,128)(2,1)S(1)}, bf16[3,128,128]{2,1,0:T(8,128)(2,1)S(1)}, u32[]{:S(2)}, u32[]{:S(2)}) collective-permute-start(bf16[3,128,128]{2,1,0:T(8,128)(2,1)S(1)} %bitcast.61), channel_id=1, source_target_pairs={{0,1},{1,0},{2,3},{3,2},{4,5},{5,4},{6,7},{7,6},{8,9},{9,8},{10,11... | collective-permute-start | bytes 294920 | tf_op jit(solution)/shard_map/ppermute | solution.py:216
  30.1 12.2 %collective-permute-start.3 = (bf16[16,2,2,16,128]{4,3,2,1,0:T(8,128)(2,1)S(1)}, bf16[16,2,2,16,128]{4,3,2,1,0:T(8,128)(2,1)S(1)}, u32[]{:S(2)}, u32[]{:S(2)}) collective-permute-start(bf16[16,2,2,16,128]{4,3,2,1,0:T(8,128)(2,1)S(1)} %all-to-all-done), channel_id=1, source_target_pairs={{0,34},{4,38},{8,42},{12,46},{16,50},{20,54},{24,58},{28,62},{1,35... | collective-permute-start | bytes 786440 | tf_op jit(solution)/shard_map/ppermute | solution.py:238
  35.3 15.0 %collective-permute-start.5 = (bf16[16,2,2,16,128]{4,3,2,1,0:T(8,128)(2,1)S(1)}, bf16[16,2,2,16,128]{4,3,2,1,0:T(8,128)(2,1)S(1)}, u32[]{:S(2)}, u32[]{:S(2)}) collective-permute-start(bf16[16,2,2,16,128]{4,3,2,1,0:T(8,128)(2,1)S(1)} %all-to-all-done), channel_id=1, source_target_pairs={{0,2},{4,6},{8,10},{12,14},{16,18},{20,22},{24,26},{28,30},{1,3},{... | collective-permute-start | bytes 786440 | tf_op jit(solution)/shard_map/ppermute | solution.py:239
  39.4 10.9 %collective-permute-start.1 = (bf16[2,3,128,128]{3,2,1,0:T(8,128)(2,1)S(1)}, bf16[2,3,128,128]{3,2,1,0:T(8,128)(2,1)S(1)}, u32[]{:S(2)}, u32[]{:S(2)}) collective-permute-start(bf16[2,3,128,128]{3,2,1,0:T(8,128)(2,1)S(1)} %pad_maximum_fusion.qa_ref), channel_id=1, source_target_pairs={{0,4},{4,0},{1,5},{5,1},{2,6},{6,2},{3,7},{7,3},{8,12},{12,8},{9,1... | collective-permute-start | bytes 589832 | tf_op jit(solution)/shard_map/ppermute | solution.py:216
  42.3 12.1 %collective-permute-start.4 = (bf16[16,2,2,16,128]{4,3,2,1,0:T(8,128)(2,1)S(1)}, bf16[16,2,2,16,128]{4,3,2,1,0:T(8,128)(2,1)S(1)}, u32[]{:S(2)}, u32[]{:S(2)}) collective-permute-start(bf16[16,2,2,16,128]{4,3,2,1,0:T(8,128)(2,1)S(1)} %collective-permute-done.3), channel_id=1, source_target_pairs={{32,34},{36,38},{40,42},{44,46},{48,50},{52,54},{56,58},{60,62},{3... | collective-permute-start | bytes 786440 | tf_op jit(solution)/shard_map/ppermute | solution.py:240
  43.0 7.3 %copy-start = (s32[3,128,128]{2,1,0:T(8,128)S(1)}, s32[3,128,128]{2,1,0:T(8,128)}, u32[]{:S(2)}) copy-start(s32[3,128,128]{2,1,0:T(8,128)} %mask_ref.3) | copy-start | bytes 589828

commit v6 on v4

--- a/solution.py
+++ b/solution.py
@@ -39,7 +39,8 @@
     pairs = []
     for c, y, z in plane_places():
         to = (y ^ bits, z) if c == 0 else (y, z ^ bits)
-        pairs.append((plane_index(c, y, z), plane_index(c, *to)))
+        if c == 1 or to[0] >= 4 or y < 4:
+            pairs.append((plane_index(c, y, z), plane_index(c, *to)))
     return pairs
 
 
@@ -234,14 +235,14 @@
     qa = jnp.stack([mine, swap(mine, "y0")])
     qb = swap(qa, "z0")
 
-    low = lax.ppermute(own, PLANE, second_axis_xor(6))
-    high = lax.ppermute(own, PLANE, second_axis_xor(2))
-    far = lax.ppermute(low, PLANE, second_axis_xor(2))
+    low = lax.ppermute(own, PLANE, second_axis_xor(2))
+    high = lax.ppermute(own, PLANE, second_axis_xor(6))
+    far = lax.ppermute(low, PLANE, second_axis_xor(6))
     own, low, high, far = (a.reshape(4, FAR, 2, 2, 16, HD) for a in (own, low, high, far))
 
     q_shards = [shard_of(y ^ (j & 1), z ^ (j >> 1)) for j in range(4)]
     k_shards = []
-    for bits in (0, 2, 6, 4):
+    for bits in (0, 6, 2, 4):
         for k in range(FAR):
             yk = jnp.where(c == 0, y ^ bits, 2 * k + y0)
             zk = jnp.where(c == 0, 2 * k + z0, z ^ bits)

time: 67.2 us -> 67.6 us (level)
  waiting for transfers between devices: 16 us -> 11.8 us
  starting transfers between devices: 32.1 us -> 34.4 us
  blocking collectives: 9.1 us -> 11.1 us
    ppermute x3, waiting for transfers between devices: 4.99 us -> 1.88 us  [swap(): return lax.ppermute(value, axis, [(0, 1), (1, 0)])]
    ppermute x3, starting transfers between devices: 12 us -> 14.2 us  [the longest x1 4.89 us: per_device(): far = lax.ppermute(low, PLANE, second_axis_xor(6))]
    all_to_all x1, blocking collectives: 9.1 us -> 11.1 us  [per_device(): parts = lax.all_to_all(parts, BLOCK, 0, 0, tiled=True)]
    ppermute x3, waiting for transfers between devices: 1.06 us -> 0.01 us  [the longest x1 0.01 us: per_device(): high = lax.ppermute(own, PLANE, second_axis_xor(6))]
  transfers between devices with their start and end apart: 7 -> 7, of which waited for: 4 -> 3; matrix products, arithmetic and copies ran while one was open for 0% -> 0% of each run, Pallas kernels for 6% -> 6%
where the time goes in v6:
time: 67.6 us; the launch traced here: 66.9 us
  starting transfers between devices  34.4 us (51%)
  waiting for transfers between devices  11.8 us (17%)
  blocking collectives  11.1 us (16%)
  Pallas kernels  7.32 us (11%)
  local copies, waits for them, and re-layouts  1.67 us (2%)
    all_to_all x1, starting transfers between devices, per_device(): lax.all_to_all(kv, AXES, 0, 0, axis_index_groups=first_axis_groups(), til...  13 us
    all_to_all x1, blocking collectives, per_device(): parts = lax.all_to_all(parts, BLOCK, 0, 0, tiled=True)  11.1 us
    all_to_all x1, waiting for transfers between devices, per_device(): lax.all_to_all(kv, AXES, 0, 0, axis_index_groups=first_axis_groups(), til...  9.95 us
    ppermute x3, starting transfers between devices, swap(): return lax.ppermute(value, axis, [(0, 1), (1, 0)])  7.24 us
    pallas_call x2, Pallas kernels, attend(): pl.pallas_call(kernel, out_shape=outs, in_specs=[pl.BlockSpec(memory_spac...  6.25 us
    ppermute x1, starting transfers between devices, per_device(): far = lax.ppermute(low, PLANE, second_axis_xor(6))  4.89 us
    ppermute x1, starting transfers between devices, per_device(): high = lax.ppermute(own, PLANE, second_axis_xor(6))  4.82 us
    ppermute x1, starting transfers between devices, per_device(): low = lax.ppermute(own, PLANE, second_axis_xor(2))  4.49 us
  transfers between devices with their start and end apart: 7, of which 3 were waited for; matrix products, arithmetic and copies ran while one was open for 0% of the time, Pallas kernels for 6%

profile of v6, /device:TPU:8, one launch (start us, length us, event | category | flops | bytes accessed | tf_op | source)
XLA Modules:
  0.0 66.9 jit_solution(7312062104049492037)
XLA Ops:
  0.0 0.8 %copy_bitcast_fusion = (bf16[1,16,8,128]{3,1,0,2:T(8,128)(2,1)S(1)}, bf16[1,16,8,128]{3,1,0,2:T(8,128)(2,1)S(1)}) fusion(bf16[1,1,16,8,128]{4,3,2,1,0:T(8,128)(2,1)} %param.6, bf16[1,1,16,8,128]{4,3,2,1,0:T(8,128)(2,1)} %param.5), kind=kLoop, calls=%fused_computation.5 | loop fusion | bytes 131072 | tf_op jit(solution)/shard_map/stack;squeeze | solution.py:223
  0.8 1.9 %collective-permute-start.2 = (bf16[4,2,16,128]{3,2,1,0:T(8,128)(2,1)S(1)}, bf16[4,2,16,128]{3,2,1,0:T(8,128)(2,1)S(1)}, u32[]{:S(2)}, u32[]{:S(2)}) collective-permute-start(bf16[4,2,16,128]{3,2,1,0:T(8,128)(2,1)S(1)} %broadcast_select_fusion), channel_id=1, source_target_pairs={{0,64},{64,0},{1,65},{65,1},{2,66},{66,2},{3,67},{67,3},{4,68},{68... | collective-permute-start | bytes 98312 | tf_op jit(solution)/shard_map/ppermute | solution.py:216
  2.8 1.2 %collective-permute-done.2 = bf16[4,2,16,128]{3,2,1,0:T(8,128)(2,1)S(1)} collective-permute-done((bf16[4,2,16,128]{3,2,1,0:T(8,128)(2,1)S(1)}, bf16[4,2,16,128]{3,2,1,0:T(8,128)(2,1)S(1)}, u32[]{:S(2)}, u32[]{:S(2)}) %collective-permute-start.2) | collective-permute-done | bytes 32800 | tf_op jit(solution)/shard_map/ppermute | solution.py:216
  4.0 0.8 %broadcast_in_dim.2 = bf16[4,4,2,2,16,128]{5,4,3,2,1,0:T(8,128)(2,1)} broadcast(bf16[4,2,2,16,128]{4,3,2,1,0:T(8,128)(2,1)S(1)} %copy.10), dimensions={0,2,3,4,5} | broadcast | bytes 327680 | tf_op jit(solution)/shard_map/broadcast_in_dim | solution.py:231
  4.7 0.0 copy-start.1
  4.7 13.0 %all-to-all-start = ((bf16[16,2,2,16,128]{4,3,2,1,0:T(8,128)(2,1)}), bf16[16,2,2,16,128]{4,3,2,1,0:T(8,128)(2,1)S(1)}, u32[]{:S(2)}, u32[]{:S(2)}) async-start(bf16[16,2,2,16,128]{4,3,2,1,0:T(8,128)(2,1)} %bitcast.34), calls=%async_computation | async-start | bytes 524288 | tf_op jit(solution)/shard_map/all_to_all | solution.py:232
  17.7 0.0 copy-done.1
  17.7 2.4 %collective-permute-start = (bf16[3,128,128]{2,1,0:T(8,128)(2,1)S(1)}, bf16[3,128,128]{2,1,0:T(8,128)(2,1)S(1)}, u32[]{:S(2)}, u32[]{:S(2)}) collective-permute-start(bf16[3,128,128]{2,1,0:T(8,128)(2,1)S(1)} %bitcast.61), channel_id=1, source_target_pairs={{0,1},{1,0},{2,3},{3,2},{4,5},{5,4},{6,7},{7,6},{8,9},{9,8},{10,11... | collective-permute-start | bytes 294920 | tf_op jit(solution)/shard_map/ppermute | solution.py:216
  20.1 9.9 %all-to-all-done = bf16[16,2,2,16,128]{4,3,2,1,0:T(8,128)(2,1)S(1)} async-done(((bf16[16,2,2,16,128]{4,3,2,1,0:T(8,128)(2,1)}), bf16[16,2,2,16,128]{4,3,2,1,0:T(8,128)(2,1)S(1)}, u32[]{:S(2)}, u32[]{:S(2)}) %all-to-all-start) | async-done | bytes 262176 | tf_op jit(solution)/shard_map/all_to_all | solution.py:232
  30.1 4.5 %collective-permute-start.3 = (bf16[16,2,2,16,128]{4,3,2,1,0:T(8,128)(2,1)S(1)}, bf16[16,2,2,16,128]{4,3,2,1,0:T(8,128)(2,1)S(1)}, u32[]{:S(2)}, u32[]{:S(2)}) collective-permute-start(bf16[16,2,2,16,128]{4,3,2,1,0:T(8,128)(2,1)S(1)} %all-to-all-done), channel_id=1, source_target_pairs={{0,2},{4,6},{8,10},{12,14},{16,18},{20,22},{24,26},{28,30},{1,3},{... | collective-permute-start | bytes 786440 | tf_op jit(solution)/shard_map/ppermute | solution.py:238
  34.6 4.8 %collective-permute-start.5 = (bf16[16,2,2,16,128]{4,3,2,1,0:T(8,128)(2,1)S(1)}, bf16[16,2,2,16,128]{4,3,2,1,0:T(8,128)(2,1)S(1)}, u32[]{:S(2)}, u32[]{:S(2)}) collective-permute-start(bf16[16,2,2,16,128]{4,3,2,1,0:T(8,128)(2,1)S(1)} %all-to-all-done), channel_id=1, source_target_pairs={{0,34},{4,38},{8,42},{12,46},{16,50},{20,54},{24,58},{28,62},{1,35... | collective-permute-start | bytes 786440 | tf_op jit(solution)/shard_map/ppermute | solution.py:239
  39.4 0.0 collective-permute-done
  39.4 3.0 %collective-permute-start.1 = (bf16[2,3,128,128]{3,2,1,0:T(8,128)(2,1)S(1)}, bf16[2,3,128,128]{3,2,1,0:T(8,128)(2,1)S(1)}, u32[]{:S(2)}, u32[]{:S(2)}) collective-permute-start(bf16[2,3,128,128]{3,2,1,0:T(8,128)(2,1)S(1)} %pad_maximum_fusion.qa_ref), channel_id=1, source_target_pairs={{0,4},{4,0},{1,5},{5,1},{2,6},{6,2},{3,7},{7,3},{8,12},{12,8},{9,1... | collective-permute-start | bytes 589832 | tf_op jit(solution)/shard_map/ppermute | solution.py:216
  42.4 0.0 collective-permute-done.3
  42.4 4.9 %collective-permute-start.4 = (bf16[16,2,2,16,128]{4,3,2,1,0:T(8,128)(2,1)S(1)}, bf16[16,2,2,16,128]{4,3,2,1,0:T(8,128)(2,1)S(1)}, u32[]{:S(2)}, u32[]{:S(2)}) collective-permute-start(bf16[16,2,2,16,128]{4,3,2,1,0:T(8,128)(2,1)S(1)} %collective-permute-done.3), channel_id=1, source_target_pairs={{0,34},{4,38},{8,42},{12,46},{16,50},{20,54},{24,58},{28,62},{1,35... | collective-permute-start | bytes 786440 | tf_op jit(solution)/shard_map/ppermute | solution.py:240
  47.3 0.0 copy-start
  47.6 0.1 stack.112.place_ref
  47.7 0.7 %collective-permute-done.1.qb_ref = bf16[2,3,128,128]{3,2,1,0:T(8,128)(2,1)S(1)} collective-permute-done((bf16[2,3,128,128]{3,2,1,0:T(8,128)(2,1)S(1)}, bf16[2,3,128,128]{3,2,1,0:T(8,128)(2,1)S(1)}, u32[]{:S(2)}, u32[]{:S(2)}) %collective-permute-start.1) | collective-permute-done | bytes 196640 | tf_op jit(solution)/shard_map/ppermute | solution.py:216
  48.4 0.0 collective-permute-done.5
  48.4 0.0 copy-done
  48.4 4.0 %attend.1 = (f32[4,384,128]{2,1,0:T(8,128)S(1)}, f32[4,384,128]{2,1,0:T(8,128)S(1)}, f32[4,384,128]{2,1,0:T(8,128)S(1)}) custom-call(s32[24]{0:T(128)S(1)} %stack.112.place_ref, bf16[2,3,128,128]{3,2,1,0:T(8,128)(2,1)S(1)} %pad_maximum_fusion.qa_ref, bf16[2,3,128,128]{3,2,1,0:T(8,128)(2,1)S(1)} %collective-permute-done.1.qb_ref, s32[3,128,128]{2,1,0:T(8,128)S(1)} %copy-done, ...), custom_call_target="tpu_custom_call" | custom-call | flops 2415919104 | bytes 1048576 | tf_op jit(solution)/shard_map/attend/pallas_call | solution.py:164
  52.5 0.0 collective-permute-done.4
  52.5 2.2 %attend_last.1 = bf16[4,400,128]{2,1,0:T(8,128)(2,1)S(1)} custom-call(s32[24]{0:T(128)S(1)} %stack.112.place_ref, bf16[2,3,128,128]{3,2,1,0:T(8,128)(2,1)S(1)} %pad_maximum_fusion.qa_ref, bf16[2,3,128,128]{3,2,1,0:T(8,128)(2,1)S(1)} %collective-permute-done.1.qb_ref, s32[3,128,128]{2,1,0:T(8,128)S(1)} %copy-done, ...), custom_call_target="tpu_custom_call" | custom-call | flops 805306368 | bytes 1048576 | tf_op jit(solution)/shard_map/attend_last/pallas_call | solution.py:164
  54.7 11.1 %all_to_all.10.p_ref = bf16[4,400,128]{2,1,0:T(8,128)(2,1)S(1)} all-to-all(bf16[4,400,128]{2,1,0:T(8,128)(2,1)S(1)} %attend_last.1), channel_id=1, replica_groups=mesh['x'=4,'c'=2,'yh'=2,'zs'=4,'z0'=2,'ys'=2,'y0'=2] {'z0','y0'}, dimensions={0} | all-to-all | bytes 819200 | tf_op jit(solution)/shard_map/all_to_all | solution.py:257
  65.8 1.1 %combine.1 = bf16[3,128,128]{2,1,0:T(8,128)(2,1)} custom-call(bf16[4,400,128]{2,1,0:T(8,128)(2,1)S(1)} %all_to_all.10.p_ref), custom_call_target="tpu_custom_call" | custom-call | tf_op jit(solution)/shard_map/combine/pallas_call | solution.py:205
  (7 shorter events, 0.1 us)
Async XLA Ops:
  0.8 3.1 %collective-permute-start.2 = (bf16[4,2,16,128]{3,2,1,0:T(8,128)(2,1)S(1)}, bf16[4,2,16,128]{3,2,1,0:T(8,128)(2,1)S(1)}, u32[]{:S(2)}, u32[]{:S(2)}) collective-permute-start(bf16[4,2,16,128]{3,2,1,0:T(8,128)(2,1)S(1)} %broadcast_select_fusion), channel_id=1, source_target_pairs={{0,64},{64,0},{1,65},{65,1},{2,66},{66,2},{3,67},{67,3},{4,68},{68... | collective-permute-start | bytes 98312 | tf_op jit(solution)/shard_map/ppermute | solution.py:216
  4.7 13.0 %copy-start.1 = (bf16[128,3,128]{2,0,1:T(8,128)(2,1)S(1)}, bf16[128,3,128]{2,0,1:T(8,128)(2,1)}, u32[]{:S(2)}) copy-start(bf16[128,3,128]{2,0,1:T(8,128)(2,1)} %param.4) | copy-start | bytes 294916
  4.7 25.3 %all-to-all-start = ((bf16[16,2,2,16,128]{4,3,2,1,0:T(8,128)(2,1)}), bf16[16,2,2,16,128]{4,3,2,1,0:T(8,128)(2,1)S(1)}, u32[]{:S(2)}, u32[]{:S(2)}) async-start(bf16[16,2,2,16,128]{4,3,2,1,0:T(8,128)(2,1)} %bitcast.34), calls=%async_computation | async-start | bytes 524288 | tf_op jit(solution)/shard_map/all_to_all | solution.py:232
  17.7 21.6 %collective-permute-start = (bf16[3,128,128]{2,1,0:T(8,128)(2,1)S(1)}, bf16[3,128,128]{2,1,0:T(8,128)(2,1)S(1)}, u32[]{:S(2)}, u32[]{:S(2)}) collective-permute-start(bf16[3,128,128]{2,1,0:T(8,128)(2,1)S(1)} %bitcast.61), channel_id=1, source_target_pairs={{0,1},{1,0},{2,3},{3,2},{4,5},{5,4},{6,7},{7,6},{8,9},{9,8},{10,11... | collective-permute-start | bytes 294920 | tf_op jit(solution)/shard_map/ppermute | solution.py:216
  30.1 12.3 %collective-permute-start.3 = (bf16[16,2,2,16,128]{4,3,2,1,0:T(8,128)(2,1)S(1)}, bf16[16,2,2,16,128]{4,3,2,1,0:T(8,128)(2,1)S(1)}, u32[]{:S(2)}, u32[]{:S(2)}) collective-permute-start(bf16[16,2,2,16,128]{4,3,2,1,0:T(8,128)(2,1)S(1)} %all-to-all-done), channel_id=1, source_target_pairs={{0,2},{4,6},{8,10},{12,14},{16,18},{20,22},{24,26},{28,30},{1,3},{... | collective-permute-start | bytes 786440 | tf_op jit(solution)/shard_map/ppermute | solution.py:238
  34.6 13.9 %collective-permute-start.5 = (bf16[16,2,2,16,128]{4,3,2,1,0:T(8,128)(2,1)S(1)}, bf16[16,2,2,16,128]{4,3,2,1,0:T(8,128)(2,1)S(1)}, u32[]{:S(2)}, u32[]{:S(2)}) collective-permute-start(bf16[16,2,2,16,128]{4,3,2,1,0:T(8,128)(2,1)S(1)} %all-to-all-done), channel_id=1, source_target_pairs={{0,34},{4,38},{8,42},{12,46},{16,50},{20,54},{24,58},{28,62},{1,35... | collective-permute-start | bytes 786440 | tf_op jit(solution)/shard_map/ppermute | solution.py:239
  39.4 9.0 %collective-permute-start.1 = (bf16[2,3,128,128]{3,2,1,0:T(8,128)(2,1)S(1)}, bf16[2,3,128,128]{3,2,1,0:T(8,128)(2,1)S(1)}, u32[]{:S(2)}, u32[]{:S(2)}) collective-permute-start(bf16[2,3,128,128]{3,2,1,0:T(8,128)(2,1)S(1)} %pad_maximum_fusion.qa_ref), channel_id=1, source_target_pairs={{0,4},{4,0},{1,5},{5,1},{2,6},{6,2},{3,7},{7,3},{8,12},{12,8},{9,1... | collective-permute-start | bytes 589832 | tf_op jit(solution)/shard_map/ppermute | solution.py:216
  42.4 10.1 %collective-permute-start.4 = (bf16[16,2,2,16,128]{4,3,2,1,0:T(8,128)(2,1)S(1)}, bf16[16,2,2,16,128]{4,3,2,1,0:T(8,128)(2,1)S(1)}, u32[]{:S(2)}, u32[]{:S(2)}) collective-permute-start(bf16[16,2,2,16,128]{4,3,2,1,0:T(8,128)(2,1)S(1)} %collective-permute-done.3), channel_id=1, source_target_pairs={{0,34},{4,38},{8,42},{12,46},{16,50},{20,54},{24,58},{28,62},{1,35... | collective-permute-start | bytes 786440 | tf_op jit(solution)/shard_map/ppermute | solution.py:240
  47.3 1.1 %copy-start = (s32[3,128,128]{2,1,0:T(8,128)S(1)}, s32[3,128,128]{2,1,0:T(8,128)}, u32[]{:S(2)}) copy-start(s32[3,128,128]{2,1,0:T(8,128)} %mask_ref.3) | copy-start | bytes 589828

commit v7 on v5

--- a/solution.py
+++ b/solution.py
@@ -167,9 +167,6 @@
         in_specs=[pl.BlockSpec(memory_space=pltpu.SMEM)] + [vmem] * (len(args) - 1),
         out_specs=[vmem] * 3 if isinstance(outs, list) else vmem,
         scratch_shapes=scratch,
-        cost_estimate=pl.CostEstimate(
-            flops=4 * 4 * QROWS * keys * HD * 2, bytes_accessed=2**20, transcendentals=4 * QROWS * keys
-        ),
         compiler_params=pltpu.CompilerParams(vmem_limit_bytes=32 * 2**20),
         name=name,
     )(*args)

time: 67.2 us -> 74 us (1.10)
  the two profiles are of different devices: /device:TPU:8 before, /device:TPU:1 now
where the time goes in v7:
time: 74 us; the launch traced here: 73.7 us
  starting transfers between devices  30.3 us (41%)
  blocking collectives  23.9 us (32%)
  waiting for transfers between devices  10.7 us (14%)
  Pallas kernels  7.31 us (10%)
  local copies, waits for them, and re-layouts  0.96 us (1%)
    ppermute x3, starting transfers between devices, swap(): return lax.ppermute(value, axis, [(0, 1), (1, 0)])  14.7 us
    all_to_all x1, blocking collectives, per_device(): lax.all_to_all(kv, AXES, 0, 0, axis_index_groups=first_axis_groups(), til...  14.5 us
    ppermute x1, starting transfers between devices, per_device(): low = lax.ppermute(own, PLANE, second_axis_xor(6))  10.5 us
    ppermute x3, waiting for transfers between devices, swap(): return lax.ppermute(value, axis, [(0, 1), (1, 0)])  9.55 us
    all_to_all x1, blocking collectives, per_device(): parts = lax.all_to_all(parts, BLOCK, 0, 0, tiled=True)  9.35 us
    pallas_call x2, Pallas kernels, attend(): pl.pallas_call(kernel, out_shape=outs, in_specs=[pl.BlockSpec(memory_spac...  6.24 us
    ppermute x1, starting transfers between devices, per_device(): far = lax.ppermute(low, PLANE, second_axis_xor(2, relay=True))  2.92 us
    ppermute x1, starting transfers between devices, per_device(): high = lax.ppermute(own, PLANE, second_axis_xor(2))  2.17 us
  transfers between devices with their start and end apart: 6, of which 3 were waited for; matrix products, arithmetic and copies ran while one was open for 0% of the time, Pallas kernels for 5%

profile of v7, /device:TPU:1, one launch (start us, length us, event | category | flops | bytes accessed | tf_op | source)
XLA Modules:
  0.0 73.7 jit_solution(13136503223202023161)
XLA Ops:
  0.0 0.8 %copy_bitcast_fusion = (bf16[1,16,8,128]{3,1,0,2:T(8,128)(2,1)S(1)}, bf16[1,16,8,128]{3,1,0,2:T(8,128)(2,1)S(1)}) fusion(bf16[1,1,16,8,128]{4,3,2,1,0:T(8,128)(2,1)} %param.6, bf16[1,1,16,8,128]{4,3,2,1,0:T(8,128)(2,1)} %param.5), kind=kLoop, calls=%fused_computation.5 | loop fusion | bytes 131072 | tf_op jit(solution)/shard_map/stack;squeeze | solution.py:220
  0.8 8.8 %collective-permute-start.2 = (bf16[4,2,16,128]{3,2,1,0:T(8,128)(2,1)S(1)}, bf16[4,2,16,128]{3,2,1,0:T(8,128)(2,1)S(1)}, u32[]{:S(2)}, u32[]{:S(2)}) collective-permute-start(bf16[4,2,16,128]{3,2,1,0:T(8,128)(2,1)S(1)} %broadcast_select_fusion), channel_id=1, source_target_pairs={{0,64},{64,0},{1,65},{65,1},{2,66},{66,2},{3,67},{67,3},{4,68},{68... | collective-permute-start | bytes 98312 | tf_op jit(solution)/shard_map/ppermute | solution.py:213
  9.6 0.8 %collective-permute-done.2 = bf16[4,2,16,128]{3,2,1,0:T(8,128)(2,1)S(1)} collective-permute-done((bf16[4,2,16,128]{3,2,1,0:T(8,128)(2,1)S(1)}, bf16[4,2,16,128]{3,2,1,0:T(8,128)(2,1)S(1)}, u32[]{:S(2)}, u32[]{:S(2)}) %collective-permute-start.2) | collective-permute-done | bytes 32800 | tf_op jit(solution)/shard_map/ppermute | solution.py:213
  10.6 0.0 copy-start.1
  10.6 14.5 %all_to_all.10 = bf16[16,2,2,16,128]{4,3,2,1,0:T(8,128)(2,1)S(1)} all-to-all(bf16[16,2,2,16,128]{4,3,2,1,0:T(8,128)(2,1)S(1)} %bitcast.59), channel_id=1, replica_groups={{0,8,16,24,128,136,144,152,256,264,272,280,384,392,400,408},{4,12,20,28..., dimensions={0} | all-to-all | bytes 524288 | tf_op jit(solution)/shard_map/all_to_all | solution.py:229
  25.1 10.5 %collective-permute-start.3 = (bf16[16,2,2,16,128]{4,3,2,1,0:T(8,128)(2,1)S(1)}, bf16[16,2,2,16,128]{4,3,2,1,0:T(8,128)(2,1)S(1)}, u32[]{:S(2)}, u32[]{:S(2)}) collective-permute-start(bf16[16,2,2,16,128]{4,3,2,1,0:T(8,128)(2,1)S(1)} %all_to_all.10), channel_id=1, source_target_pairs={{0,34},{4,38},{8,42},{12,46},{16,50},{20,54},{24,58},{28,62},{1,35... | collective-permute-start | bytes 786440 | tf_op jit(solution)/shard_map/ppermute | solution.py:235
  35.6 0.0 copy-done.1
  35.6 2.8 %collective-permute-start = (bf16[3,128,128]{2,1,0:T(8,128)(2,1)S(1)}, bf16[3,128,128]{2,1,0:T(8,128)(2,1)S(1)}, u32[]{:S(2)}, u32[]{:S(2)}) collective-permute-start(bf16[3,128,128]{2,1,0:T(8,128)(2,1)S(1)} %bitcast.62), channel_id=1, source_target_pairs={{0,1},{1,0},{2,3},{3,2},{4,5},{5,4},{6,7},{7,6},{8,9},{9,8},{10,11... | collective-permute-start | bytes 294920 | tf_op jit(solution)/shard_map/ppermute | solution.py:213
  38.5 2.2 %collective-permute-start.5 = (bf16[16,2,2,16,128]{4,3,2,1,0:T(8,128)(2,1)S(1)}, bf16[16,2,2,16,128]{4,3,2,1,0:T(8,128)(2,1)S(1)}, u32[]{:S(2)}, u32[]{:S(2)}) collective-permute-start(bf16[16,2,2,16,128]{4,3,2,1,0:T(8,128)(2,1)S(1)} %all_to_all.10), channel_id=1, source_target_pairs={{0,2},{4,6},{8,10},{12,14},{16,18},{20,22},{24,26},{28,30},{1,3},{... | collective-permute-start | bytes 786440 | tf_op jit(solution)/shard_map/ppermute | solution.py:236
  40.6 1.1 %collective-permute-done.3 = bf16[16,2,2,16,128]{4,3,2,1,0:T(8,128)(2,1)S(1)} collective-permute-done((bf16[16,2,2,16,128]{4,3,2,1,0:T(8,128)(2,1)S(1)}, bf16[16,2,2,16,128]{4,3,2,1,0:T(8,128)(2,1)S(1)}, u32[]{:S(2)}, u32[]{:S(2)}) %collective-permute-start.3) | collective-permute-done | bytes 262176 | tf_op jit(solution)/shard_map/ppermute | solution.py:235
  41.7 2.9 %collective-permute-start.4 = (bf16[16,2,2,16,128]{4,3,2,1,0:T(8,128)(2,1)S(1)}, bf16[16,2,2,16,128]{4,3,2,1,0:T(8,128)(2,1)S(1)}, u32[]{:S(2)}, u32[]{:S(2)}) collective-permute-start(bf16[16,2,2,16,128]{4,3,2,1,0:T(8,128)(2,1)S(1)} %collective-permute-done.3), channel_id=1, source_target_pairs={{32,34},{36,38},{40,42},{44,46},{48,50},{52,54},{56,58},{60,62},{3... | collective-permute-start | bytes 786440 | tf_op jit(solution)/shard_map/ppermute | solution.py:237
  44.7 0.0 collective-permute-done
  44.7 3.1 %collective-permute-start.1 = (bf16[2,3,128,128]{3,2,1,0:T(8,128)(2,1)S(1)}, bf16[2,3,128,128]{3,2,1,0:T(8,128)(2,1)S(1)}, u32[]{:S(2)}, u32[]{:S(2)}) collective-permute-start(bf16[2,3,128,128]{3,2,1,0:T(8,128)(2,1)S(1)} %pad_maximum_fusion.qa_ref), channel_id=1, source_target_pairs={{0,4},{4,0},{1,5},{5,1},{2,6},{6,2},{3,7},{7,3},{8,12},{12,8},{9,1... | collective-permute-start | bytes 589832 | tf_op jit(solution)/shard_map/ppermute | solution.py:213
  47.8 0.0 copy-start
  48.1 0.1 stack.112.place_ref
  48.2 8.7 %collective-permute-done.1.qb_ref = bf16[2,3,128,128]{3,2,1,0:T(8,128)(2,1)S(1)} collective-permute-done((bf16[2,3,128,128]{3,2,1,0:T(8,128)(2,1)S(1)}, bf16[2,3,128,128]{3,2,1,0:T(8,128)(2,1)S(1)}, u32[]{:S(2)}, u32[]{:S(2)}) %collective-permute-start.1) | collective-permute-done | bytes 196640 | tf_op jit(solution)/shard_map/ppermute | solution.py:213
  57.0 0.0 collective-permute-done.5
  57.0 0.0 copy-done
  57.0 4.0 %attend.1 = (f32[4,384,128]{2,1,0:T(8,128)S(1)}, f32[4,384,128]{2,1,0:T(8,128)S(1)}, f32[4,384,128]{2,1,0:T(8,128)S(1)}) custom-call(s32[24]{0:T(128)S(1)} %stack.112.place_ref, bf16[2,3,128,128]{3,2,1,0:T(8,128)(2,1)S(1)} %pad_maximum_fusion.qa_ref, bf16[2,3,128,128]{3,2,1,0:T(8,128)(2,1)S(1)} %collective-permute-done.1.qb_ref, s32[3,128,128]{2,1,0:T(8,128)S(1)} %copy-done, ...), custom_call_target="tpu_custom_call" | custom-call | tf_op jit(solution)/shard_map/attend/pallas_call | solution.py:164
  61.0 0.0 collective-permute-done.4
  61.0 2.2 %attend_last.1 = bf16[4,400,128]{2,1,0:T(8,128)(2,1)S(1)} custom-call(s32[24]{0:T(128)S(1)} %stack.112.place_ref, bf16[2,3,128,128]{3,2,1,0:T(8,128)(2,1)S(1)} %pad_maximum_fusion.qa_ref, bf16[2,3,128,128]{3,2,1,0:T(8,128)(2,1)S(1)} %collective-permute-done.1.qb_ref, s32[3,128,128]{2,1,0:T(8,128)S(1)} %copy-done, ...), custom_call_target="tpu_custom_call" | custom-call | tf_op jit(solution)/shard_map/attend_last/pallas_call | solution.py:164
  63.2 9.4 %all_to_all.11.p_ref = bf16[4,400,128]{2,1,0:T(8,128)(2,1)S(1)} all-to-all(bf16[4,400,128]{2,1,0:T(8,128)(2,1)S(1)} %attend_last.1), channel_id=1, replica_groups=mesh['x'=4,'c'=2,'yh'=2,'zs'=4,'z0'=2,'ys'=2,'y0'=2] {'z0','y0'}, dimensions={0} | all-to-all | bytes 819200 | tf_op jit(solution)/shard_map/all_to_all | solution.py:254
  72.6 1.1 %combine.1 = bf16[3,128,128]{2,1,0:T(8,128)(2,1)} custom-call(bf16[4,400,128]{2,1,0:T(8,128)(2,1)S(1)} %all_to_all.11.p_ref), custom_call_target="tpu_custom_call" | custom-call | tf_op jit(solution)/shard_map/combine/pallas_call | solution.py:202
  (8 shorter events, 0.1 us)
Async XLA Ops:
  0.8 9.6 %collective-permute-start.2 = (bf16[4,2,16,128]{3,2,1,0:T(8,128)(2,1)S(1)}, bf16[4,2,16,128]{3,2,1,0:T(8,128)(2,1)S(1)}, u32[]{:S(2)}, u32[]{:S(2)}) collective-permute-start(bf16[4,2,16,128]{3,2,1,0:T(8,128)(2,1)S(1)} %broadcast_select_fusion), channel_id=1, source_target_pairs={{0,64},{64,0},{1,65},{65,1},{2,66},{66,2},{3,67},{67,3},{4,68},{68... | collective-permute-start | bytes 98312 | tf_op jit(solution)/shard_map/ppermute | solution.py:213
  10.6 25.1 %copy-start.1 = (bf16[128,3,128]{2,0,1:T(8,128)(2,1)S(1)}, bf16[128,3,128]{2,0,1:T(8,128)(2,1)}, u32[]{:S(2)}) copy-start(bf16[128,3,128]{2,0,1:T(8,128)(2,1)} %param.4) | copy-start | bytes 294916
  25.1 16.6 %collective-permute-start.3 = (bf16[16,2,2,16,128]{4,3,2,1,0:T(8,128)(2,1)S(1)}, bf16[16,2,2,16,128]{4,3,2,1,0:T(8,128)(2,1)S(1)}, u32[]{:S(2)}, u32[]{:S(2)}) collective-permute-start(bf16[16,2,2,16,128]{4,3,2,1,0:T(8,128)(2,1)S(1)} %all_to_all.10), channel_id=1, source_target_pairs={{0,34},{4,38},{8,42},{12,46},{16,50},{20,54},{24,58},{28,62},{1,35... | collective-permute-start | bytes 786440 | tf_op jit(solution)/shard_map/ppermute | solution.py:235
  35.6 9.0 %collective-permute-start = (bf16[3,128,128]{2,1,0:T(8,128)(2,1)S(1)}, bf16[3,128,128]{2,1,0:T(8,128)(2,1)S(1)}, u32[]{:S(2)}, u32[]{:S(2)}) collective-permute-start(bf16[3,128,128]{2,1,0:T(8,128)(2,1)S(1)} %bitcast.62), channel_id=1, source_target_pairs={{0,1},{1,0},{2,3},{3,2},{4,5},{5,4},{6,7},{7,6},{8,9},{9,8},{10,11... | collective-permute-start | bytes 294920 | tf_op jit(solution)/shard_map/ppermute | solution.py:213
  38.5 18.5 %collective-permute-start.5 = (bf16[16,2,2,16,128]{4,3,2,1,0:T(8,128)(2,1)S(1)}, bf16[16,2,2,16,128]{4,3,2,1,0:T(8,128)(2,1)S(1)}, u32[]{:S(2)}, u32[]{:S(2)}) collective-permute-start(bf16[16,2,2,16,128]{4,3,2,1,0:T(8,128)(2,1)S(1)} %all_to_all.10), channel_id=1, source_target_pairs={{0,2},{4,6},{8,10},{12,14},{16,18},{20,22},{24,26},{28,30},{1,3},{... | collective-permute-start | bytes 786440 | tf_op jit(solution)/shard_map/ppermute | solution.py:236
  41.7 19.3 %collective-permute-start.4 = (bf16[16,2,2,16,128]{4,3,2,1,0:T(8,128)(2,1)S(1)}, bf16[16,2,2,16,128]{4,3,2,1,0:T(8,128)(2,1)S(1)}, u32[]{:S(2)}, u32[]{:S(2)}) collective-permute-start(bf16[16,2,2,16,128]{4,3,2,1,0:T(8,128)(2,1)S(1)} %collective-permute-done.3), channel_id=1, source_target_pairs={{32,34},{36,38},{40,42},{44,46},{48,50},{52,54},{56,58},{60,62},{3... | collective-permute-start | bytes 786440 | tf_op jit(solution)/shard_map/ppermute | solution.py:237
  44.7 12.3 %collective-permute-start.1 = (bf16[2,3,128,128]{3,2,1,0:T(8,128)(2,1)S(1)}, bf16[2,3,128,128]{3,2,1,0:T(8,128)(2,1)S(1)}, u32[]{:S(2)}, u32[]{:S(2)}) collective-permute-start(bf16[2,3,128,128]{3,2,1,0:T(8,128)(2,1)S(1)} %pad_maximum_fusion.qa_ref), channel_id=1, source_target_pairs={{0,4},{4,0},{1,5},{5,1},{2,6},{6,2},{3,7},{7,3},{8,12},{12,8},{9,1... | collective-permute-start | bytes 589832 | tf_op jit(solution)/shard_map/ppermute | solution.py:213
  47.8 9.1 %copy-start = (s32[3,128,128]{2,1,0:T(8,128)S(1)}, s32[3,128,128]{2,1,0:T(8,128)}, u32[]{:S(2)}) copy-start(s32[3,128,128]{2,1,0:T(8,128)} %mask_ref.3) | copy-start | bytes 589828
